TPU v7x, 256 devices: a whole 4x4x8 slice. The times are simulated.
256 devices in a mesh: dp: 16 (over z_lo, x), ctx: 16 (over y, z_hi, core).
Axes of the slice: x: 4, y: 4, z: 8 (z_hi: 2, z_lo: 4; z = z_hi * 4 + z_lo), core: 2. Of those that a mesh axis runs over, the one named last changes fastest.
Arguments:
- queries: bfloat16 [32768, 32, 128], P(('dp', 'ctx')), may hold values from -8 to 8
- keys: bfloat16 [32768, 4, 128], P(('dp', 'ctx')), may hold values from -8 to 8
- values: bfloat16 [32768, 4, 128], P(('dp', 'ctx')), may hold values from -6 to 6
- out_grad: bfloat16 [32768, 32, 128], P(('dp', 'ctx')), may hold values from -6 to 6
- q_gain: float32 [128], replicated, may hold values from 0.5 to 5
- k_gain: float32 [128], replicated, may hold values from 0.5 to 5
- lengths: int32 [16, 8], P('dp'), may hold values from 1 to 1025, 2048 in all within a row
- prompt_ids: int32 [16, 8], replicated, may hold values from 0 to 15, as said below
- grades: int32 [16, 8], replicated, may hold values from 0 to 3
Outputs:
- q_grad: bfloat16 [32768, 32, 128], P(('dp', 'ctx'))
- k_grad: bfloat16 [32768, 4, 128], P(('dp', 'ctx'))
- v_grad: bfloat16 [32768, 4, 128], P(('dp', 'ctx'))
- q_gain_grad: float32 [128], replicated
- k_gain_grad: float32 [128], replicated
Inputs may be any that keep to these rules, and one draw needn't show every extreme that they name: Each row's lengths sum to 2048; the longest response of each row has 1025 tokens. `prompt_ids`: every id names exactly 8 responses.
All inputs are finite; a program needn't handle non-finite values.
Results may differ from a plain program's by a relative error of at most 0.004.
The roundings to bfloat16 on the way count: a program that leaves them out, or rounds other values in their place, can miss the bound.
Values may be sent and summed in bfloat16 or wider, within the bound.
No kernel may reach another device: no remote copies, remote signals or barrier semaphores. Data moves between devices by JAX's collectives and lax.ppermute only.
A program may use at most 128 MiB of HBM per device.

v0:
```python
import math

import jax
import jax.numpy as jnp
from jax import lax
from jax.sharding import PartitionSpec as P

norm_eps = 1e-06


def layout(lens, row_length):
    ends = jnp.cumsum(lens)
    starts = ends - lens
    index = jnp.arange(row_length, dtype=jnp.int32)
    member = jnp.sum((index[:, None] >= ends[None, :]).astype(jnp.int32), axis=1)
    owners = member[:, None] == jnp.arange(lens.shape[0], dtype=jnp.int32)[None, :]
    opening = jnp.sum(jnp.where(owners, starts[None, :], 0), axis=1)
    return (member, opening)


def advantages(grades, prompt_ids):
    graded = grades.reshape(-1).astype(jnp.float32)
    labels = prompt_ids.reshape(-1)
    same = (labels[:, None] == labels[None, :]).astype(jnp.float32)
    counted = jnp.sum(same, axis=1)
    centre = jnp.sum(same * graded[None, :], axis=1) / counted
    spread = graded[None, :] - centre[:, None]
    variance = jnp.sum(same * spread * spread, axis=1) / counted
    return ((graded - centre) / jnp.maximum(jnp.sqrt(variance), 1.0)).reshape(grades.shape)


def rope_tables(positions, head_width):
    half = head_width // 2
    freqs = jnp.power(1000000.0, -(jnp.arange(half, dtype=jnp.float32) * (2.0 / head_width)))
    angles = positions.astype(jnp.float32)[:, None] * freqs[None, :]
    cosine = jnp.cos(angles)
    sine = jnp.sin(angles)
    return (jnp.concatenate([cosine, cosine], axis=1), jnp.concatenate([sine, sine], axis=1))


def norm_rope(inputs, gain, cosine, sine):
    values_f = inputs.astype(jnp.float32)
    inv_rms = lax.rsqrt(jnp.mean(values_f * values_f, axis=-1, keepdims=True) + norm_eps)
    normed = values_f * inv_rms * gain
    half = inputs.shape[-1] // 2
    turned = jnp.concatenate([-normed[..., half:], normed[..., :half]], axis=-1)
    return (normed * cosine[:, None, :] + turned * sine[:, None, :]).astype(jnp.bfloat16)


def unrotate(inputs, gain, cosine, sine, incoming):
    half = inputs.shape[-1] // 2
    along = incoming * cosine[:, None, :]
    across = incoming * sine[:, None, :]
    d_normed = along - jnp.concatenate([-across[..., half:], across[..., :half]], axis=-1)
    values_f = inputs.astype(jnp.float32)
    inv_rms = lax.rsqrt(jnp.mean(values_f * values_f, axis=-1, keepdims=True) + norm_eps)
    unit = values_f * inv_rms
    gain_term = jnp.sum(d_normed * unit, axis=(0, 1))
    upper = d_normed * gain
    result = inv_rms * (upper - unit * jnp.mean(upper * unit, axis=-1, keepdims=True))
    return (result.astype(jnp.bfloat16), gain_term)


def attention_grads(
    query_tile,
    grad_tile,
    key_rows,
    value_rows,
    query_member,
    query_index,
    key_member,
    tile_size,
    first_tile,
    last_tile,
    key_accum,
    value_accum,
):
    query_count, kv_count, group_count, head_width = query_tile.shape
    inv_root = 1.0 / math.sqrt(head_width)

    def make_tile(tile_index):
        opening = tile_index * tile_size
        key_tile = lax.dynamic_slice_in_dim(key_rows, opening, tile_size, 0)
        value_tile = lax.dynamic_slice_in_dim(value_rows, opening, tile_size, 0)
        tile_member = lax.dynamic_slice_in_dim(key_member, opening, tile_size, 0)
        key_index = opening + jnp.arange(tile_size, dtype=jnp.int32)
        allowed = (tile_member[None, :] == query_member[:, None]) & (
            key_index[None, :] <= query_index[:, None]
        )
        allowed = allowed[:, None, None, :]
        score = (
            jnp.einsum("qhgd,khd->qhgk", query_tile, key_tile, preferred_element_type=jnp.float32)
            * inv_root
        )
        d_prob = jnp.einsum(
            "qhgd,khd->qhgk", grad_tile, value_tile, preferred_element_type=jnp.float32
        )
        return (opening, key_tile, allowed, score, d_prob)

    def forward_pass(tile_index, running):
        running_max, running_sum, running_dot = running
        opening, key_tile, allowed, score, d_prob = make_tile(tile_index)
        masked = jnp.where(allowed, score, -1e30)
        new_max = jnp.maximum(running_max, jnp.max(masked, axis=-1))
        decay = jnp.exp(running_max - new_max)
        prob = jnp.where(allowed, jnp.exp(masked - new_max[..., None]), 0.0)
        return (
            new_max,
            running_sum * decay + jnp.sum(prob, axis=-1),
            running_dot * decay + jnp.sum(prob * d_prob, axis=-1),
        )

    shape_rows = (query_count, kv_count, group_count)
    start_state = (
        jnp.full(shape_rows, -1e30, jnp.float32),
        jnp.zeros(shape_rows, jnp.float32),
        jnp.zeros(shape_rows, jnp.float32),
    )
    running_max, running_sum, running_dot = lax.fori_loop(
        first_tile, last_tile, forward_pass, start_state
    )
    log_total = running_max + jnp.log(running_sum)
    d_total = running_dot / running_sum

    def backward_pass(tile_index, running):
        query_accum, key_sum, value_sum = running
        opening, key_tile, allowed, score, d_prob = make_tile(tile_index)
        prob = jnp.where(
            allowed, jnp.exp(jnp.where(allowed, score, -1e30) - log_total[..., None]), 0.0
        )
        d_score = (prob * (d_prob - d_total[..., None])).astype(jnp.bfloat16)
        prob_b = prob.astype(jnp.bfloat16)
        value_tile_grad = jnp.einsum(
            "qhgk,qhgd->khd", prob_b, grad_tile, preferred_element_type=jnp.float32
        )
        key_tile_grad = (
            jnp.einsum("qhgk,qhgd->khd", d_score, query_tile, preferred_element_type=jnp.float32)
            * inv_root
        )
        query_accum = (
            query_accum
            + jnp.einsum("qhgk,khd->qhgd", d_score, key_tile, preferred_element_type=jnp.float32)
            * inv_root
        )
        key_old = lax.dynamic_slice_in_dim(key_sum, opening, tile_size, 0)
        key_sum = lax.dynamic_update_slice_in_dim(key_sum, key_old + key_tile_grad, opening, 0)
        value_old = lax.dynamic_slice_in_dim(value_sum, opening, tile_size, 0)
        value_sum = lax.dynamic_update_slice_in_dim(
            value_sum, value_old + value_tile_grad, opening, 0
        )
        return (query_accum, key_sum, value_sum)

    query_start = jnp.zeros(query_tile.shape, jnp.float32)
    return lax.fori_loop(
        first_tile, last_tile, backward_pass, (query_start, key_accum, value_accum)
    )


def on_device(queries, keys, values, out_grad, q_gain, k_gain, lengths, prompt_ids, grades):
    own_rows, query_heads, head_width = queries.shape
    kv_heads = keys.shape[1]
    ctx_count = lax.axis_size("ctx")
    ctx_place = lax.axis_index("ctx")
    row_place = lax.axis_index("dp")
    row_length = own_rows * ctx_count
    member_all, opening_all = layout(lengths[0], row_length)
    own_offset = ctx_place * own_rows
    own_member = lax.dynamic_slice_in_dim(member_all, own_offset, own_rows, 0)
    own_index = own_offset + jnp.arange(own_rows, dtype=jnp.int32)
    own_opening = lax.dynamic_slice_in_dim(opening_all, own_offset, own_rows, 0)
    adv = advantages(grades, prompt_ids)
    selector = (jnp.arange(adv.shape[0], dtype=jnp.int32) == row_place).astype(jnp.float32)
    row_adv = jnp.sum(selector[:, None] * adv, axis=0)
    owners = own_member[:, None] == jnp.arange(adv.shape[1], dtype=jnp.int32)[None, :]
    weight = jnp.sum(jnp.where(owners, row_adv[None, :], 0.0), axis=1)
    dout = (weight[:, None, None] * out_grad.astype(jnp.float32)).astype(jnp.bfloat16)
    cosine, sine = rope_tables(own_index - own_opening, head_width)
    q_rot = norm_rope(queries, q_gain, cosine, sine)
    k_rot = norm_rope(keys, k_gain, cosine, sine)
    tile_size = math.gcd(row_length, 256)
    group_size = query_heads // kv_heads
    key_all, value_all = (
        lax.all_gather(k_rot, "ctx", axis=0, tiled=True),
        lax.all_gather(values, "ctx", axis=0, tiled=True),
    )
    first_tile = jnp.min(own_opening) // tile_size
    last_tile = (own_offset + own_rows - 1) // tile_size + 1
    empty_rows = jnp.zeros((row_length, kv_heads, head_width), jnp.float32)
    query_part, key_rows_grad, value_rows_grad = attention_grads(
        q_rot.reshape(own_rows, kv_heads, group_size, head_width),
        dout.reshape(own_rows, kv_heads, group_size, head_width),
        key_all,
        value_all,
        own_member,
        own_index,
        member_all,
        tile_size,
        first_tile,
        last_tile,
        empty_rows,
        empty_rows,
    )
    dk_own, dv_own = (
        lax.psum_scatter(key_rows_grad, "ctx", scatter_dimension=0, tiled=True),
        lax.psum_scatter(value_rows_grad, "ctx", scatter_dimension=0, tiled=True),
    )
    dq_full = query_part.reshape(own_rows, query_heads, head_width)
    q_grad, q_term = unrotate(queries, q_gain, cosine, sine, dq_full)
    k_grad, k_term = unrotate(keys, k_gain, cosine, sine, dk_own)
    q_total, k_total = lax.psum((q_term, k_term), ("dp", "ctx"))
    return (q_grad, k_grad, dv_own.astype(jnp.bfloat16), q_total, k_total)


def solution(mesh):
    in_specs = (
        P(("dp", "ctx"), None, None),
        P(("dp", "ctx"), None, None),
        P(("dp", "ctx"), None, None),
        P(("dp", "ctx"), None, None),
        P(),
        P(),
        P("dp", None),
        P(),
        P(),
    )
    out_specs = (
        P(("dp", "ctx"), None, None),
        P(("dp", "ctx"), None, None),
        P(("dp", "ctx"), None, None),
        P(),
        P(),
    )
    return jax.shard_map(
        on_device, mesh=mesh, in_specs=in_specs, out_specs=out_specs, check_vma=False
    )
```

profile of v0, /device:TPU:1, one launch (start us, length us, event | category | flops | bytes accessed | tf_op | source)
XLA Modules:
  0.0 703.0 jit_solution(14792981757663327837)
XLA Ops:
  9.0 1.1 fusion.67
  10.1 1.1 fusion.61
  12.7 1.0 fusion.69
  19.4 1.3 fusion.57
  22.7 1.4 copy.58
  25.3 55.7 %all-gather.3.cloned.1.call-done = bf16[2048,4,128]{2,1,0:T(4,128)(2,1)} async-done(((bf16[128,4,128]{2,1,0:T(4,128)(2,1)}), bf16[2048,4,128]{2,1,0:T(4,128)(2,1)}) %all-gather.3.cloned.1.call-update) | async-done | bytes 2097168 | tf_op jit(solution)/shard_map/all_gather | solution.py:183
  81.1 1.9 copy.61
  82.9 60.0 %all-gather.5.cloned.1.call-done = bf16[2048,4,128]{2,0,1:T(8,128)(2,1)} async-done(((bf16[128,4,128]{2,0,1:T(8,128)(2,1)}), bf16[2048,4,128]{2,0,1:T(8,128)(2,1)}) %all-gather.5.cloned.1.call-update) | async-done | bytes 2097168 | tf_op jit(solution)/shard_map/all_gather | solution.py:184
  144.2 8.1 %while.30 = (s32[]{:T(128)}, f32[128,4,8]{0,2,1:T(8,128)S(1)}, f32[128,4,8]{0,2,1:T(8,128)}, f32[128,4,8]{0,2,1:T(8,128)}, s32[]{:T(128)}, /*index=5*/s32[2048]{...) while((s32[]{:T(128)}, f32[128,4,8]{0,2,1:T(8,128)S(1)}, ...), condition=%wide.region_15.16_spmd.clone, body=%wide.region_11.15_spmd.clone.sunk | while | flops 551661952 | bytes 20093804 | solution.py:119
  148.1 2.3 fusion.108
  150.5 1.1 fusion.109
  152.2 1.4 fusion.75
  153.9 2.2 broadcast_in_dim.81.clone
  156.1 2.2 broadcast_in_dim.81.clone2
  158.4 12.9 %while.31 = (s32[]{:T(128)}, f32[128,4,8,128]{0,3,2,1:T(8,128)S(1)}, f32[2048,4,128]{2,1,0:T(4,128)}, f32[2048,4,128]{2,1,0:T(4,128)}, s32[]{:T(128)}, /*index=5...) while((s32[]{:T(128)}, ...), condition=%wide.region_17.18_spmd.clone, body=%wide.region_16.17_spmd.clone.sunk | while | flops 1356300672 | bytes 38820692 | solution.py:154
  158.4 1.7 fusion.120
  161.1 2.5 fusion.121
  163.6 1.9 bitcast_add_fusion.2
  165.5 1.1 constant_dynamic-slice_fusion.4
  166.6 1.1 fusion.122
  167.7 1.1 constant_dynamic-slice_fusion.5
  169.5 1.7 copy_dynamic-update-slice_fusion.3
  171.3 2.0 copy.63
  173.3 348.8 %all-reduce.7 = bf16[2048,4,128]{2,1,0:T(4,128)(2,1)} all-reduce(f32[2048,4,128]{2,1,0:T(4,128)} %get-tuple-element.150), channel_id=3, replica_groups=mesh['dp'=16,'ctx'=16] {'ctx'}, use_global_device_ids=true, to_apply=%region_21.22.clone | all-reduce | flops 1048576 | bytes 6291456
  522.1 1.6 dynamic-slice_convert_fusion
  525.3 1.8 fusion.53
  527.2 2.5 fusion.52
  529.7 55.9 %all-reduce.6.cloned.1.call-done = f32[2048,4,128]{2,1,0:T(4,128)} async-done(((f32[2048,4,128]{2,1,0:T(4,128)}), f32[2048,4,128]{2,1,0:T(4,128)}) %all-reduce.6.cloned.1.call-update) | async-done | bytes 4194320
  585.6 1.0 dynamic-slice_multiply_fusion
  586.8 1.5 fusion.66
  588.3 1.0 fusion.65
  589.3 107.2 %all-reduce.2 = (f32[128]{0:T(128)}, f32[128]{0:T(128)}) all-reduce(f32[128]{0:T(128)S(1)} %get-tuple-element.315, f32[128]{0:T(128)S(1)} %get-tuple-element.317), channel_id=1, replica_groups=mesh['dp'=16,'ctx'=16] {'dp','ctx'}, use_global_device_ids=true, to_apply=%region_23.24 | all-reduce | flops 256 | bytes 2048 | tf_op jit(solution)/shard_map/psum | solution.py:210
  (111 shorter events, 18.2 us)
Async XLA Ops:
  7.2 5.5 copy-start.4
  7.2 5.5 copy-start.18
  7.2 6.6 copy-start.12
  7.2 10.0 %copy-start = (bf16[128,32,128]{2,1,0:T(8,128)(2,1)S(1)}, bf16[128,32,128]{2,1,0:T(8,128)(2,1)}, u32[]{:S(2)}) copy-start(bf16[128,32,128]{2,1,0:T(8,128)(2,1)} %param.13) | copy-start | bytes 3145732
  7.2 73.9 %all-gather.3.cloned.1.call-start = ((), (), s32[]{:S(2)}) async-start(), calls=%async_computation | async-start | bytes 2228224 | tf_op jit(solution)/shard_map/all_gather | solution.py:183
  9.0 8.9 %copy-start.13 = (s32[2048]{0:T(1024)}, s32[2048]{0:T(1024)S(1)}, u32[]{:S(2)}) copy-start(s32[2048]{0:T(1024)S(1)} %convert_reduce_fusion) | copy-start | bytes 24580
  11.3 6.6 copy-start.20
  13.7 129.2 %all-gather.5.cloned.1.call-start = ((), (), s32[]{:S(2)}) async-start(), calls=%async_computation.1 | async-start | bytes 2228224 | tf_op jit(solution)/shard_map/all_gather | solution.py:184
  14.5 571.1 %all-reduce.6.cloned.1.call-start = ((), (), s32[]{:S(2)}) async-start(), calls=%async_computation.2 | async-start | bytes 8388608
  17.2 5.1 copy-start.14
  20.6 0.7 copy-start.22
  20.6 0.8 copy-start.23
  20.6 1.8 copy-start.5
  22.4 1.7 copy-start.24
  146.9 1.2 copy-start.6
  150.5 1.1 copy-start.8
  150.5 1.1 copy-start.10
  151.6 0.6 copy-start.9
  151.6 0.6 copy-start.11
  152.2 1.4 copy-start.3
  156.1 2.3 copy-start.15
  158.4 2.7 copy-start.7
  158.4 2.7 copy-start.16
  158.4 2.7 copy-start.17
  173.3 350.4 %copy-start.2 = (f32[128,4,8,128]{3,2,1,0:T(8,128)S(1)}, f32[128,4,8,128]{3,2,1,0:T(8,128)}, u32[]{:S(2)}) copy-start(f32[128,4,8,128]{3,2,1,0:T(8,128)} %copy.63) | copy-start | bytes 6291460
  524.1 1.2 copy-start.1
  524.1 1.2 copy-start.21
  527.2 59.6 %copy-start.19 = (f32[128]{0:T(128)S(1)}, f32[128]{0:T(128)}, u32[]{:S(2)}) copy-start(f32[128]{0:T(128)} %param.18) | copy-start | bytes 1540
Sparse Core Ops, SparseCore 0:
  13.9 67.1 all-gather.2
  84.4 58.5 all-gather.4
  173.4 412.1 all-reduce.5
where the time goes:
time: 704 us; the launch traced here: 703 us
  blocking collectives  456 us (65%)
  waiting for transfers between devices  172 us (24%)
  other arithmetic  24.3 us (3%)
  local copies, waits for them, and re-layouts  22.3 us (3%)
  between operations  17.3 us (2%)
  matrix products  11 us (2%)
    unnamed x1, blocking collectives  349 us
    psum x1, blocking collectives, on_device(): q_total, k_total = lax.psum((q_term, k_term), ('dp', 'ctx'))  107 us
    all_gather x1, waiting for transfers between devices, on_device(): lax.all_gather(values, 'ctx', axis=0, tiled=True)  60 us
    unnamed x4, waiting for transfers between devices  55.9 us
    all_gather x1, waiting for transfers between devices, on_device(): lax.all_gather(k_rot, 'ctx', axis=0, tiled=True)  55.7 us
  transfers between devices with their start and end apart: 3, of which 3 were waited for; matrix products, arithmetic and copies ran while one was open for 2% of the time, Pallas kernels for 0%

commit v1 on v0

v1 whole, which is shorter than its diff:
```python
import functools
import math

import jax
import jax.numpy as jnp
from jax import lax
from jax.experimental import pallas as pl
from jax.experimental.pallas import tpu as pltpu
from jax.sharding import PartitionSpec as P

EPS = 1e-06
TOK = 128
HD = 128
BLK = 2 * TOK
REACH = 4
GROUP = 8
HEADS = 2
SLOTS = HEADS * 2 * (GROUP // 2)
ROOT = 1.0 / math.sqrt(HD)
EXP_SCALE = ROOT * math.log2(math.e)
MASKED = -1e30
QMAX = 32000.0
VMEM = pltpu.CompilerParams(vmem_limit_bytes=56 * 1024 * 1024)

f32, bf16, i32 = jnp.float32, jnp.bfloat16, jnp.int32


def dot(a, b, dims):
    return lax.dot_general(a, b, (dims, ((), ())), preferred_element_type=f32)


def inv_rms(x):
    return lax.rsqrt(jnp.mean(x * x, axis=-1, keepdims=True) + EPS)


def turn(x):
    return pltpu.roll(x, HD // 2, x.ndim - 1)


def norm_rope(x, gain, cosine, sine):
    xn = x * inv_rms(x) * gain
    return xn * cosine + turn(xn) * sine


def unrotate(x, gain, cosine, sine, incoming):
    dn = incoming * cosine - turn(incoming) * sine
    r = inv_rms(x)
    unit = x * r
    u = dn * gain
    grad = r * (u - unit * jnp.mean(u * unit, axis=-1, keepdims=True))
    return grad, jnp.sum(dn * unit, axis=0, keepdims=True)


def token_base(place, k, half):
    chip, core = place // 2, place % 2
    return ((chip - k) * 2 + (core if half == 0 else 1 - core)) * TOK


def openings(idx, lens):
    total = jnp.int32(0)
    out = jnp.zeros_like(idx)
    for j in range(lens.shape[1]):
        total = total + lens[0, j]
        out = jnp.where(idx >= total, total, out)
    return out


def needed(place, k, half, lens):
    base = token_base(place, 0, half)
    total, first = jnp.int32(0), jnp.int32(0)
    for j in range(lens.shape[1]):
        total = total + lens[0, j]
        first = jnp.where(base >= total, total, first)
    low = (place // 2 - k) * BLK
    return (low >= 0) & (low + BLK > first)


def fill_bias(bias, place, k, half, lens):
    qidx = token_base(place, 0, half) + lax.broadcasted_iota(i32, (1, TOK), 1)
    start = openings(qidx, lens)
    for part in range(2):
        kidx = token_base(place, k, part) + lax.broadcasted_iota(i32, (TOK, TOK), 0)
        good = (kidx <= qidx) & (kidx >= start)
        row = jnp.where(good, 0.0, MASKED)
        bias[part * TOK : (part + 1) * TOK, :] = jnp.concatenate([row, row], axis=1)


def place_of():
    return lax.axis_index("ctx")


def prep_kernel(
    lens, ids_s, grades_s, ids, grades, q_own, q_other, g_own, g_other, gain, cosine, sine, q_out, g_out
):
    place, row, core = place_of(), lax.axis_index("dp"), lax.axis_index("ctx") % 2
    gain_row = gain[...]
    adv = []
    pid, grd = ids[...], grades[...].astype(f32)
    for j in range(lens.shape[1]):
        same = jnp.where(pid == ids_s[row, j], 1.0, 0.0)
        count = jnp.sum(same, keepdims=True)
        centre = jnp.sum(same * grd, keepdims=True) / count
        spread = grd - centre
        variance = jnp.sum(same * spread * spread, keepdims=True) / count
        own = grades_s[row, j].astype(f32)
        adv.append((own - centre) / jnp.maximum(jnp.sqrt(variance), 1.0))
    for half in range(2):
        idx = token_base(place, 0, half) + lax.broadcasted_iota(i32, (TOK, HD), 0)
        weight = jnp.zeros((TOK, HD), f32)
        total = jnp.int32(0)
        for j in range(lens.shape[1]):
            weight = jnp.where(idx >= total, adv[j], weight)
            total = total + lens[0, j]
        cos_h = cosine[0, half * TOK : (half + 1) * TOK, :]
        sin_h = sine[0, half * TOK : (half + 1) * TOK, :]

        def body(pair, carry):
            head, two = pair // (GROUP // 2), pair % (GROUP // 2)
            slot = (head * 2 + half) * (GROUP // 2) + two
            for e in range(2):
                n = pair * 2 + e
                if half == 0:
                    x, g = q_own[core, n], g_own[core, n]
                else:
                    x, g = q_other[n], g_other[n]
                rot = norm_rope(x.astype(f32), gain_row, cos_h, sin_h)
                q_out[slot, e * TOK : (e + 1) * TOK, :] = rot.astype(bf16)
                g_out[slot, e * TOK : (e + 1) * TOK, :] = (weight * g.astype(f32)).astype(bf16)
            return carry

        lax.fori_loop(0, HEADS * GROUP // 2, body, 0)


def rotate_keys(kv, gain_row, cosine, sine, kr):
    for half in range(2):
        rows = slice(half * TOK, (half + 1) * TOK)
        for head in range(HEADS):
            x = kv[half, 0, head].astype(f32)
            kr[head, rows, :] = norm_rope(x, gain_row, cosine[rows, :], sine[rows, :]).astype(bf16)


def join_values(kv, vv):
    for half in range(2):
        for head in range(HEADS):
            vv[head, half * TOK : (half + 1) * TOK, :] = kv[half, 1, head]


def forward_kernel(blocks, has_state, *refs):
    lens, gain, cosine, sine, q, g = refs[:6]
    rest = refs[6:]
    kvs, rest = rest[: len(blocks)], rest[len(blocks) :]
    if has_state:
        old, rest = rest[:3], rest[3:]
    (m, l, d), (kr, vv, bias) = rest[:3], rest[3:]
    place = place_of()
    gain_row = gain[...]
    if has_state:
        m[...], l[...], d[...] = old[0][...], old[1][...], old[2][...]
    else:
        m[...] = jnp.full(m.shape, MASKED, f32)
        l[...] = jnp.zeros(l.shape, f32)
        d[...] = jnp.zeros(d.shape, f32)
    for k, kv in zip(blocks, kvs):
        rotate_keys(kv, gain_row, cosine.at[k], sine.at[k], kr)
        join_values(kv, vv)
        for half in range(2):

            @pl.when(needed(place, k, half, lens))
            def _():
                fill_bias(bias, place, k, half, lens)

                def body(it, carry):
                    head, two = it // (GROUP // 2), it % (GROUP // 2)
                    slot = (head * 2 + half) * (GROUP // 2) + two
                    s = dot(kr[head], q[slot], ((1,), (1,))) + bias[...]
                    dp = dot(vv[head], g[slot], ((1,), (1,)))
                    m_old = m[slot]
                    m_new = jnp.maximum(m_old, jnp.max(s, axis=0, keepdims=True))
                    e = jnp.exp2((s - m_new) * EXP_SCALE)
                    fade = jnp.exp2((m_old - m_new) * EXP_SCALE)
                    m[slot] = m_new
                    l[slot] = l[slot] * fade + jnp.sum(e, axis=0, keepdims=True)
                    d[slot] = d[slot] * fade + jnp.sum(e * dp, axis=0, keepdims=True)
                    return carry

                lax.fori_loop(0, HEADS * GROUP // 2, body, 0)


def code(dk, dv, packed):
    rows = lax.broadcasted_iota(i32, (16, HD), 0)
    marks = jnp.zeros((16, HD), f32)
    for kind, ref in enumerate((dk, dv)):
        for head in range(HEADS):
            x = ref[head]
            peak = jnp.maximum(jnp.max(jnp.abs(x), axis=0, keepdims=True), 1e-30)
            mark = jnp.ceil(jnp.log2(peak) * 256.0)
            n = kind * HEADS + head
            marks = jnp.where(rows == n, mark, marks)
            fixed = x * (jnp.exp2(mark * (-1.0 / 256.0)) * QMAX)
            packed[n * BLK : (n + 1) * BLK, :] = (
                jnp.floor(fixed + 0.5).astype(i32).astype(jnp.int16)
            )
    packed[2 * HEADS * BLK :, :] = marks.astype(i32).astype(jnp.int16)


def backward_kernel(blocks, has_dq, last, *refs):
    lens, gain, cosine, sine, q, g, m, l, d = refs[:9]
    rest = refs[9:]
    kvs, rest = rest[: len(blocks)], rest[len(blocks) :]
    if has_dq:
        dq_in, term_in, rest = rest[0], rest[1], rest[2:]
    if last:
        (q_own, q_other, q_gain), rest = rest[:3], rest[3:]
        (q_grad, terms, dk_own, dv_own), rest = rest[:4], rest[4:]
        dq, kr, vv, krt, bias, dk, dv, lse, mean_d = rest
        packs = ()
    else:
        (dq, terms), rest = rest[:2], rest[2:]
        packs, rest = rest[: len(blocks)], rest[len(blocks) :]
        kr, vv, krt, bias, dk, dv, lse, mean_d = rest
    place, core = place_of(), lax.axis_index("ctx") % 2
    gain_row = gain[...]
    if has_dq:
        dq[...] = dq_in[...]
        terms[...] = term_in[...]
    else:
        dq[...] = jnp.zeros(dq.shape, f32)
        terms[...] = jnp.zeros(terms.shape, f32)
    lse[...] = m[...] * EXP_SCALE + jnp.log2(l[...])
    mean_d[...] = d[...] / l[...]
    for n, (k, kv) in enumerate(zip(blocks, kvs)):
        if last:
            dk, dv = dk_own, dv_own
        dk[...] = jnp.zeros(dk.shape, f32)
        dv[...] = jnp.zeros(dv.shape, f32)
        rotate_keys(kv, gain_row, cosine.at[k], sine.at[k], kr)
        join_values(kv, vv)
        for head in range(HEADS):
            krt[head] = jnp.transpose(kr[head].astype(f32)).astype(bf16)
        for half in range(2):

            @pl.when(needed(place, k, half, lens))
            def _():
                fill_bias(bias, place, k, half, lens)

                def body(it, carry):
                    head, two = it // (GROUP // 2), it % (GROUP // 2)
                    slot = (head * 2 + half) * (GROUP // 2) + two
                    s = dot(kr[head], q[slot], ((1,), (1,))) + bias[...]
                    dp = dot(vv[head], g[slot], ((1,), (1,)))
                    p = jnp.exp2(s * EXP_SCALE - lse[slot])
                    ds = (p * (dp - mean_d[slot])).astype(bf16)
                    dv[head] += dot(p.astype(bf16), g[slot], ((1,), (0,)))
                    dk[head] += dot(ds, q[slot], ((1,), (0,)))
                    dq[slot] += dot(krt[head], ds, ((1,), (0,)))
                    return carry

                lax.fori_loop(0, HEADS * GROUP // 2, body, 0)

        total = jnp.zeros((1, HD), f32)
        for half in range(2):
            rows = slice(half * TOK, (half + 1) * TOK)
            for head in range(HEADS):
                x = kv[half, 0, head].astype(f32)
                dn = (
                    dk[head, rows, :] * cosine[k, rows, :] - turn(dk[head, rows, :]) * sine[k, rows, :]
                )
                total = total + jnp.sum(dn * (x * inv_rms(x)), axis=0, keepdims=True)
        terms[1:2, :] = terms[1:2, :] + total * ROOT
        if not last:
            code(dk, dv, packs[n])
    if last:
        for half in range(2):
            cos_h = cosine[0, half * TOK : (half + 1) * TOK, :]
            sin_h = sine[0, half * TOK : (half + 1) * TOK, :]

            def finish(pair, total):
                head, two = pair // (GROUP // 2), pair % (GROUP // 2)
                slot = (head * 2 + half) * (GROUP // 2) + two
                incoming = jnp.transpose(dq[slot]) * ROOT
                for e in range(2):
                    n = pair * 2 + e
                    x = (q_own[core, n] if half == 0 else q_other[n]).astype(f32)
                    grad, part = unrotate(
                        x, q_gain[...], cos_h, sin_h, incoming[e * TOK : (e + 1) * TOK, :]
                    )
                    q_grad[half, n] = grad.astype(bf16)
                    total = total + part
                return total

            total = lax.fori_loop(0, HEADS * GROUP // 2, finish, jnp.zeros((1, HD), f32))
            terms[0:1, :] = terms[0:1, :] + total


def finish_kernel(gain, cosine, sine, kv, dk, dv, p1, p2, p3, p4, out):
    gain_row = gain[...]
    packs = (p1, p2, p3, p4)
    marks = [p[2 * HEADS * BLK :, :].astype(i32).astype(f32) for p in packs]
    for kind, ref in enumerate((dk, dv)):
        for head in range(HEADS):
            n = kind * HEADS + head
            scales = [jnp.exp2(k[n : n + 1, :] * (1.0 / 256.0)) * (1.0 / QMAX) for k in marks]
            for half in range(2):
                rows = slice(half * TOK, (half + 1) * TOK)
                total = ref[head, rows, :]
                for p, scale in zip(packs, scales):
                    at = n * BLK + half * TOK
                    total = total + p[at : at + TOK, :].astype(i32).astype(f32) * scale
                if kind == 0:
                    x = kv[half, 0, head].astype(f32)
                    total, _ = unrotate(
                        x, gain_row, cosine[0, rows, :], sine[0, rows, :], total * ROOT
                    )
                out[half, kind, head] = total.astype(bf16)


def vmem(count):
    return [pl.BlockSpec(memory_space=pltpu.VMEM)] * count


def smem(count):
    return [pl.BlockSpec(memory_space=pltpu.SMEM)] * count


def block_scratch():
    return [
        pltpu.VMEM((HEADS, BLK, HD), bf16),
        pltpu.VMEM((HEADS, BLK, HD), bf16),
    ]


def bias_scratch():
    return pltpu.VMEM((BLK, BLK), f32)


STAT = jax.ShapeDtypeStruct((SLOTS, 1, BLK), f32)


def cost(units, flops):
    return pl.CostEstimate(
        flops=units * flops, bytes_accessed=4 << 20, transcendentals=units * BLK * BLK
    )


def forward(blocks, lens, gain, cosine, sine, q, g, kvs, state):
    has_state = state is not None
    args = [lens, gain, cosine, sine, q, g, *kvs, *(state or ())]
    return pl.pallas_call(
        functools.partial(forward_kernel, blocks, has_state),
        out_shape=[STAT] * 3,
        in_specs=smem(1) + vmem(len(args) - 1),
        out_specs=vmem(3),
        scratch_shapes=block_scratch() + [bias_scratch()],
        compiler_params=VMEM,
        cost_estimate=cost(16 * len(blocks), 4 * BLK * BLK * HD),
        name="forward" + "".join(map(str, blocks)),
    )(*args)


def backward(blocks, lens, gain, cosine, sine, q, g, state, kvs, carried, final):
    has_dq, last = carried is not None, final is not None
    args = [lens, gain, cosine, sine, q, g, *state, *kvs, *(carried or ()), *(final or ())]
    dq = (SLOTS, HD, BLK)
    terms = jax.ShapeDtypeStruct((8, HD), f32)
    grads = (HEADS, BLK, HD)
    scratch = block_scratch() + [pltpu.VMEM((HEADS, HD, BLK), bf16), bias_scratch()]
    scratch += [pltpu.VMEM(grads, f32)] * 2 + [pltpu.VMEM((SLOTS, 1, BLK), f32)] * 2
    if last:
        out_shape = [
            jax.ShapeDtypeStruct((2, HEADS * GROUP, TOK, HD), bf16),
            terms,
            jax.ShapeDtypeStruct(grads, f32),
            jax.ShapeDtypeStruct(grads, f32),
        ]
        scratch = [pltpu.VMEM(dq, f32)] + scratch
    else:
        packed = jax.ShapeDtypeStruct((2 * HEADS * BLK + 16, HD), jnp.int16)
        out_shape = [jax.ShapeDtypeStruct(dq, f32), terms] + [packed] * len(blocks)
    return pl.pallas_call(
        functools.partial(backward_kernel, blocks, has_dq, last),
        out_shape=out_shape,
        in_specs=smem(1) + vmem(len(args) - 1),
        out_specs=vmem(len(out_shape)),
        scratch_shapes=scratch,
        compiler_params=VMEM,
        cost_estimate=cost(16 * len(blocks), 10 * BLK * BLK * HD),
        name="backward" + "".join(map(str, blocks)),
    )(*args)


def rope_tables(place, lens):
    chip, core = place // 2, place % 2
    k = jnp.arange(REACH + 1, dtype=i32)[:, None, None]
    half = jnp.arange(2, dtype=i32)[None, :, None]
    t = jnp.arange(TOK, dtype=i32)[None, None, :]
    index = (((chip - k) * 2 + jnp.where(half == 0, core, 1 - core)) * TOK + t).reshape(
        REACH + 1, BLK
    )
    tri = jnp.arange(lens.shape[1])
    ends = jnp.sum(jnp.where(tri[None, :] <= tri[:, None], lens[0][None, :], 0), axis=1)
    start = jnp.max(jnp.where(index[..., None] >= ends, ends, 0), axis=-1)
    freqs = jnp.power(1000000.0, -(jnp.arange(HD // 2, dtype=f32) * (2.0 / HD)))
    angles = (index - start).astype(f32)[..., None] * freqs
    cosine, sine = jnp.cos(angles), jnp.sin(angles)
    return (
        jnp.concatenate([cosine, cosine], axis=-1),
        jnp.concatenate([-sine, sine], axis=-1),
    )


def swap_cores(x):
    return lax.ppermute(x, "ctx", [(i, i ^ 1) for i in range(16)])


def shift_chips(x, k):
    return lax.ppermute(x, "ctx", [(i, i + 2 * k) for i in range(16) if 0 <= i + 2 * k < 16])


def on_device(queries, keys, values, out_grad, q_gain, k_gain, lengths, prompt_ids, grades):
    place = lax.axis_index("ctx")
    core = place % 2
    q_gain2, k_gain2 = q_gain.reshape(1, HD), k_gain.reshape(1, HD)

    kv = jnp.stack([keys, values]).transpose(2, 0, 1, 3).reshape(2, HEADS, 2, TOK, HD)
    kv = kv.transpose(0, 2, 1, 3, 4)
    kv_mine = lax.dynamic_index_in_dim(kv, core, 0, keepdims=False)
    kv_other = swap_cores(lax.dynamic_index_in_dim(kv, 1 - core, 0, keepdims=False))
    own = jnp.stack([kv_mine, kv_other])
    blocks = [own] + [shift_chips(own, k) for k in range(1, REACH + 1)]

    heads = HEADS * GROUP
    q_t = queries.transpose(1, 0, 2).reshape(2, heads, TOK, HD)
    g_t = out_grad.transpose(1, 0, 2).reshape(2, heads, TOK, HD)
    q_other = swap_cores(lax.dynamic_index_in_dim(q_t, 1 - core, 0, keepdims=False))
    g_other = swap_cores(lax.dynamic_index_in_dim(g_t, 1 - core, 0, keepdims=False))
    cosine, sine = rope_tables(place, lengths)

    rows = jax.ShapeDtypeStruct((SLOTS, BLK, HD), bf16)
    q, g = pl.pallas_call(
        prep_kernel,
        out_shape=[rows, rows],
        in_specs=smem(3) + vmem(9),
        out_specs=vmem(2),
        compiler_params=VMEM,
        name="prepare",
    )(
        lengths, prompt_ids, grades, prompt_ids, grades,
        q_t, q_other, g_t, g_other, q_gain2, cosine, sine,
    )

    common = (lengths, k_gain2, cosine, sine, q, g)
    state = forward((0,), *common, blocks[:1], None)
    state = forward((1, 2, 3, 4), *common, blocks[1:], state)
    dq, terms, pack4, pack3 = backward((4, 3), *common, state, [blocks[4], blocks[3]], None, None)
    back4, back3 = shift_chips(pack4, -4), shift_chips(pack3, -3)
    dq, terms, pack2, pack1 = backward(
        (2, 1), *common, state, [blocks[2], blocks[1]], (dq, terms), None
    )
    back2, back1 = shift_chips(pack2, -2), shift_chips(pack1, -1)
    q_half, terms, dk, dv = backward(
        (0,), *common, state, blocks[:1], (dq, terms), (q_t, q_other, q_gain2)
    )

    q_swapped = swap_cores(q_half[1])
    first = jnp.where(core == 0, q_half[0], q_swapped)
    second = jnp.where(core == 0, q_swapped, q_half[0])
    q_grad = jnp.concatenate([first, second]).transpose(1, 0, 2)

    pair = terms[:2].reshape(1, 2 * HD)
    count = lax.axis_size("dp") * lax.axis_size("ctx")
    gathered = lax.all_to_all(
        jnp.broadcast_to(pair, (count, 2 * HD)), ("dp", "ctx"), 0, 0, tiled=True
    )
    gains = jnp.sum(gathered, axis=0)

    out = pl.pallas_call(
        finish_kernel,
        out_shape=jax.ShapeDtypeStruct((2, 2, HEADS, TOK, HD), bf16),
        in_specs=vmem(10),
        out_specs=vmem(1)[0],
        compiler_params=VMEM,
        name="finish",
    )(k_gain2, cosine, sine, own, dk, dv, back1, back2, back3, back4)
    mine, other = out[0], swap_cores(out[1])
    first = jnp.where(core == 0, mine, other)
    second = jnp.where(core == 0, other, mine)
    kv_grad = jnp.concatenate([first, second], axis=1).transpose(0, 2, 1, 3)
    return (q_grad, kv_grad[0], kv_grad[1], gains[:HD], gains[HD:])


def solution(mesh):
    rows = P(("dp", "ctx"), None, None)
    return jax.shard_map(
        on_device,
        mesh=mesh,
        in_specs=(rows, rows, rows, rows, P(), P(), P("dp", None), P(), P()),
        out_specs=(rows, rows, rows, P(), P()),
        check_vma=False,
    )
```

time: 704 us -> 167 us (0.24)
  blocking collectives: 456 us -> 0 us
  waiting for transfers between devices: 172 us -> 5.92 us
  starting transfers between devices: 0.12 us -> 87.4 us
  Pallas kernels: 0 us -> 53.9 us
  other arithmetic: 24.3 us -> 5.61 us
  between operations: 17.3 us -> 1.04 us
  matrix products: 11 us -> 0 us
  local copies, waits for them, and re-layouts: 22.3 us -> 12.3 us
    unnamed x1 -> x0, blocking collectives: 349 us -> none
    all_gather x2 -> x0, waiting for transfers between devices: 116 us -> none  [the longest x1 60 us: on_device(): lax.all_gather(values, 'ctx', axis=0, tiled=True)]
    psum x1 -> x0, blocking collectives: 107 us -> none  [on_device(): q_total, k_total = lax.psum((q_term, k_term), ('dp', 'ctx'))]
    all_to_all x0 -> x1, starting transfers between devices: none -> 57.7 us  [on_device(): lax.all_to_all(jnp.broadcast_to(pair, (count, 2 * HD)), ('dp', 'ctx'), 0,...]
    unnamed x4 -> x0, waiting for transfers between devices: 55.9 us -> none
    pallas_call x0 -> x7, Pallas kernels: none -> 53.9 us  [the longest x3 30.4 us: backward(): pl.pallas_call(functools.partial(backward_kernel, blocks, has_dq, last),...]
    ppermute x0 -> x13, starting transfers between devices: none -> 29.7 us  [the longest x8 23.4 us: shift_chips(): lax.ppermute(x, 'ctx', [(i, i + 2 * k) for i in range(16) if 0 <= i + 2 *...]
    dot_general x7 -> x0, matrix products: 11 us -> none  [the longest x2 4.82 us: make_tile(): jnp.einsum('qhgd,khd->qhgk', grad_tile, value_tile, preferred_element_typ...]
  transfers between devices with their start and end apart: 3 -> 14, of which waited for: 3 -> 2; matrix products, arithmetic and copies ran while one was open for 2% -> 8% of each run, Pallas kernels for 0% -> 23%
where the time goes in v1:
time: 167 us; the launch traced here: 166 us
  starting transfers between devices  87.4 us (52%)
  Pallas kernels  53.9 us (32%)
  local copies, waits for them, and re-layouts  12.3 us (7%)
  waiting for transfers between devices  5.92 us (4%)
  other arithmetic  5.61 us (3%)
    all_to_all x1, starting transfers between devices, on_device(): lax.all_to_all(jnp.broadcast_to(pair, (count, 2 * HD)), ('dp', 'ctx'), 0,...  57.7 us
    pallas_call x3, Pallas kernels, backward(): pl.pallas_call(functools.partial(backward_kernel, blocks, has_dq, last),...  30.4 us
    ppermute x8, starting transfers between devices, shift_chips(): lax.ppermute(x, 'ctx', [(i, i + 2 * k) for i in range(16) if 0 <= i + 2 *...  23.4 us
    pallas_call x2, Pallas kernels, forward(): pl.pallas_call(functools.partial(forward_kernel, blocks, has_state), out_...  12.3 us
    pallas_call x1, Pallas kernels, on_device(): pl.pallas_call(prep_kernel, out_shape=[rows, rows], in_specs=smem(3) + vm...  7.99 us
    unnamed x40, local copies, waits for them, and re-layouts  6.4 us
    ppermute x5, starting transfers between devices, swap_cores(): return lax.ppermute(x, 'ctx', [(i, i ^ 1) for i in range(16)])  6.29 us
    all_to_all x1, waiting for transfers between devices, on_device(): lax.all_to_all(jnp.broadcast_to(pair, (count, 2 * HD)), ('dp', 'ctx'), 0,...  5.07 us
  transfers between devices with their start and end apart: 14, of which 2 were waited for; matrix products, arithmetic and copies ran while one was open for 8% of the time, Pallas kernels for 23%

profile of v1, /device:TPU:1, one launch (start us, length us, event | category | flops | bytes accessed | tf_op | source)
XLA Modules:
  0.0 166.2 jit_solution(15085303349539792757)
XLA Ops:
  0.7 1.1 copy_bitcast_fusion.2
  1.9 3.3 %collective-permute-start.2 = (bf16[2,2,128,128]{3,2,1,0:T(8,128)(2,1)S(1)}, bf16[2,2,128,128]{3,2,1,0:T(8,128)(2,1)S(1)}, u32[]{:S(2)}, u32[]{:S(2)}) collective-permute-start(bf16[2,2,128,128]{3,2,1,0:T(8,128)(2,1)S(1)} %bitcast.67), channel_id=1, source_target_pairs={{0,1},{1,0},{2,3},{3,2},{4,5},{5,4},{6,7},{7,6},{8,9},{9,8},{10,11... | collective-permute-start | bytes 393224 | tf_op jit(solution)/shard_map/ppermute | solution.py:412
  6.2 0.8 dynamic-slice_bitcast_fusion
  8.1 3.8 %collective-permute-start.6 = (bf16[2,2,2,128,128]{4,3,2,1,0:T(8,128)(2,1)S(1)}, bf16[2,2,2,128,128]{4,3,2,1,0:T(8,128)(2,1)}, u32[]{:S(2)}, u32[]{:S(2)}) collective-permute-start(bf16[2,2,2,128,128]{4,3,2,1,0:T(8,128)(2,1)S(1)} %pad_maximum_fusion.3.refs_6_.refs_9_.kv), channel_id=1, source_target_pairs={{0,8},{1,9},{2,10},{3,11},{4,12},{5,13},{6,14},{7,15},{16,24},{17,... | collective-permute-start | bytes 786440 | tf_op jit(solution)/shard_map/ppermute | solution.py:416
  11.9 9.6 %collective-permute-start.5 = (bf16[2,2,2,128,128]{4,3,2,1,0:T(8,128)(2,1)S(1)}, bf16[2,2,2,128,128]{4,3,2,1,0:T(8,128)(2,1)}, u32[]{:S(2)}, u32[]{:S(2)}) collective-permute-start(bf16[2,2,2,128,128]{4,3,2,1,0:T(8,128)(2,1)S(1)} %pad_maximum_fusion.3.refs_6_.refs_9_.kv), channel_id=1, source_target_pairs={{0,6},{1,7},{2,8},{3,9},{4,10},{5,11},{6,12},{7,13},{8,14},{9,15},... | collective-permute-start | bytes 786440 | tf_op jit(solution)/shard_map/ppermute | solution.py:416
  21.5 2.0 %collective-permute-start.4 = (bf16[2,2,2,128,128]{4,3,2,1,0:T(8,128)(2,1)S(1)}, bf16[2,2,2,128,128]{4,3,2,1,0:T(8,128)(2,1)}, u32[]{:S(2)}, u32[]{:S(2)}) collective-permute-start(bf16[2,2,2,128,128]{4,3,2,1,0:T(8,128)(2,1)S(1)} %pad_maximum_fusion.3.refs_6_.refs_9_.kv), channel_id=1, source_target_pairs={{0,4},{1,5},{2,6},{3,7},{4,8},{5,9},{6,10},{7,11},{8,12},{9,13},{1... | collective-permute-start | bytes 786440 | tf_op jit(solution)/shard_map/ppermute | solution.py:416
  23.5 0.8 copy-done.3
  24.4 2.8 %collective-permute-start.3 = (bf16[2,2,2,128,128]{4,3,2,1,0:T(8,128)(2,1)S(1)}, bf16[2,2,2,128,128]{4,3,2,1,0:T(8,128)(2,1)}, u32[]{:S(2)}, u32[]{:S(2)}) collective-permute-start(bf16[2,2,2,128,128]{4,3,2,1,0:T(8,128)(2,1)S(1)} %pad_maximum_fusion.3.refs_6_.refs_9_.kv), channel_id=1, source_target_pairs={{0,2},{1,3},{2,4},{3,5},{4,6},{5,7},{6,8},{7,9},{8,10},{9,11},{10,... | collective-permute-start | bytes 786440 | tf_op jit(solution)/shard_map/ppermute | solution.py:416
  27.2 2.4 %fusion = (f32[5,256,64]{2,1,0:T(8,128)S(1)}, f32[5,256,64]{2,1,0:T(8,128)S(1)}, f32[5,256,64]{2,1,0:T(8,128)S(1)}) fusion(f32[64]{0:T(128)S(1)} %negate_power_fusion, f32[5,256]{1,0:T(8,128)S(1)} %subtract_convert_fusion), kind=kLoop, calls=%fused_computation.13 | loop fusion | flops 163840 | bytes 988416 | tf_op jit(solution)/shard_map/neg | solution.py:407
  30.9 1.5 pad_maximum_fusion
  32.4 8.0 %prepare.1 = (bf16[16,256,128]{2,1,0:T(8,128)(2,1)}, bf16[16,256,128]{2,1,0:T(8,128)(2,1)}) custom-call(s32[1,8]{1,0:T(1,128)} %refs_0_.9, s32[16,8]{1,0:T(8,128)} %copy.51.ids_s.ids, s32[16,8]{1,0:T(8,128)} %copy.52.grades_s.grades, s32[16,8]{1,0:T(8,128)} %copy.51.ids_s.ids, s32[16,8]{1,0:T(8,128)} %copy.52.grades_s.grades, ...), custom_call_target="tpu_custom_call" | custom-call | tf_op jit(solution)/shard_map/prepare/pallas_call | solution.py:439
  40.4 8.1 %forward0.1 = (f32[16,1,256]{2,1,0:T(1,128)}, f32[16,1,256]{2,1,0:T(1,128)}, f32[16,1,256]{2,1,0:T(1,128)}) custom-call(s32[1,8]{1,0:T(1,128)} %refs_0_.9, f32[1,128]{1,0:T(1,128)} %bitcast.70, f32[5,256,128]{2,1,0:T(8,128)} %get-tuple-element.78.cosine.refs_2_, f32[5,256,128]{2,1,0:T(8,128)} %get-tuple-element.79.sine.refs_3_, ...), custom_call_target="tpu_custom_call" | custom-call | flops 536870912 | bytes 4194304 | tf_op jit(solution)/shard_map/forward0/pallas_call | solution.py:348
  48.5 4.3 %forward1234.1 = (f32[16,1,256]{2,1,0:T(1,128)}, f32[16,1,256]{2,1,0:T(1,128)}, f32[16,1,256]{2,1,0:T(1,128)}) custom-call(s32[1,8]{1,0:T(1,128)} %refs_0_.9, f32[1,128]{1,0:T(1,128)} %bitcast.71, f32[5,256,128]{2,1,0:T(8,128)} %get-tuple-element.78.cosine.refs_2_, f32[5,256,128]{2,1,0:T(8,128)} %get-tuple-element.79.sine.refs_3_, ...), custom_call_target="tpu_custom_call" | custom-call | flops 2147483648 | bytes 4194304 | tf_op jit(solution)/shard_map/forward1234/pallas_call | solution.py:348
  52.7 5.2 %backward43.1 = (f32[16,128,256]{2,1,0:T(8,128)}, f32[8,128]{1,0:T(8,128)}, s16[1040,128]{1,0:T(8,128)(2,1)}, s16[1040,128]{1,0:T(8,128)(2,1)}) custom-call(s32[1,8]{1,0:T(1,128)} %refs_0_.9, f32[1,128]{1,0:T(1,128)} %bitcast.72, f32[5,256,128]{2,1,0:T(8,128)} %get-tuple-element.78.cosine.refs_2_, f32[5,256,128]{2,1,0:T(8,128)} %get-tuple-element.79.sine.refs_3_, ...), custom_call_target="tpu_custom_call" | custom-call | flops 2684354560 | bytes 4194304 | tf_op jit(solution)/shard_map/backward43/pallas_call | solution.py:379
  57.9 5.8 %backward21.1 = (f32[16,128,256]{2,1,0:T(8,128)}, f32[8,128]{1,0:T(8,128)}, s16[1040,128]{1,0:T(8,128)(2,1)}, s16[1040,128]{1,0:T(8,128)(2,1)}) custom-call(s32[1,8]{1,0:T(1,128)} %refs_0_.9, f32[1,128]{1,0:T(1,128)} %bitcast.73, f32[5,256,128]{2,1,0:T(8,128)} %get-tuple-element.78.cosine.refs_2_, f32[5,256,128]{2,1,0:T(8,128)} %get-tuple-element.79.sine.refs_3_, ...), custom_call_target="tpu_custom_call" | custom-call | flops 2684354560 | bytes 4194304 | tf_op jit(solution)/shard_map/backward21/pallas_call | solution.py:379
  63.7 1.3 collective-permute-start.8
  65.0 1.3 collective-permute-start.9
  66.3 1.3 collective-permute-start.10
  67.6 1.3 collective-permute-start.11
  68.9 19.5 %backward0.1 = (bf16[2,16,128,128]{3,2,1,0:T(8,128)(2,1)}, f32[8,128]{1,0:T(8,128)}, f32[2,256,128]{2,1,0:T(8,128)}, f32[2,256,128]{2,1,0:T(8,128)}) custom-call(s32[1,8]{1,0:T(1,128)} %refs_0_.9, f32[1,128]{1,0:T(1,128)} %bitcast.74, f32[5,256,128]{2,1,0:T(8,128)} %get-tuple-element.78.cosine.refs_2_, f32[5,256,128]{2,1,0:T(8,128)} %get-tuple-element.79.sine.refs_3_, ...), custom_call_target="tpu_custom_call" | custom-call | flops 1342177280 | bytes 4194304 | tf_op jit(solution)/shard_map/backward0/pallas_call | solution.py:379
  88.4 0.7 slice_bitcast_fusion.5
  89.1 0.9 broadcast_in_dim.50
  90.0 57.7 %all-to-all-start = ((f32[256,1,256]{2,1,0:T(1,128)}), f32[256,1,256]{2,1,0:T(1,128)S(1)}, u32[]{:S(2)}, u32[]{:S(2)}) async-start(f32[256,1,256]{2,1,0:T(1,128)} %broadcast_in_dim.50), calls=%async_computation | async-start | bytes 524288 | tf_op jit(solution)/shard_map/all_to_all | solution.py:471
  148.7 3.2 %finish.1 = bf16[2,2,2,128,128]{4,3,2,1,0:T(8,128)(2,1)} custom-call(f32[1,128]{1,0:T(1,128)} %bitcast.75, f32[5,256,128]{2,1,0:T(8,128)} %get-tuple-element.78.cosine.refs_2_, f32[5,256,128]{2,1,0:T(8,128)} %get-tuple-element.79.sine.refs_3_, bf16[2,2,2,128,128]{4,3,2,1,0:T(8,128)(2,1)} %copy-done.2, f32[2,256,128]{2,1,0:T(8,128)} %get-tuple-element.38.dk, ...), custom_call_target="tpu_custom_call" | custom-call | tf_op jit(solution)/shard_map/finish/pallas_call | solution.py:476
  151.8 0.9 slice_bitcast_fusion.3
  152.8 2.2 %collective-permute-start.12 = (bf16[2,2,128,128]{3,2,1,0:T(8,128)(2,1)S(1)}, bf16[2,2,128,128]{3,2,1,0:T(8,128)(2,1)S(1)}, u32[]{:S(2)}, u32[]{:S(2)}) collective-permute-start(bf16[2,2,128,128]{3,2,1,0:T(8,128)(2,1)S(1)} %slice_bitcast_fusion.3), channel_id=1, source_target_pairs={{0,1},{1,0},{2,3},{3,2},{4,5},{5,4},{6,7},{7,6},{8,9},{9,8},{10,11... | collective-permute-start | bytes 393224 | tf_op jit(solution)/shard_map/ppermute | solution.py:412
  155.2 0.8 collective-permute-done.12
  156.0 0.9 broadcast_select_fusion.1
  157.0 0.8 copy.62
  157.7 0.8 copy.61
  158.5 5.1 %all-to-all-done = f32[256,1,256]{2,1,0:T(1,128)S(1)} async-done(((f32[256,1,256]{2,1,0:T(1,128)}), f32[256,1,256]{2,1,0:T(1,128)S(1)}, u32[]{:S(2)}, u32[]{:S(2)}) %all-to-all-start) | async-done | bytes 262176 | tf_op jit(solution)/shard_map/all_to_all | solution.py:471
  164.6 1.6 copy.60
  (73 shorter events, 5.5 us)
Async XLA Ops:
  0.6 4.6 %copy-start.5 = (bf16[128,32,128]{2,1,0:T(8,128)(2,1)S(1)}, bf16[128,32,128]{2,1,0:T(8,128)(2,1)}, u32[]{:S(2)}) copy-start(bf16[128,32,128]{2,1,0:T(8,128)(2,1)} %param.9) | copy-start | bytes 3145732
  1.8 4.0 %copy-start.6 = (bf16[128,32,128]{2,1,0:T(8,128)(2,1)S(1)}, bf16[128,32,128]{2,1,0:T(8,128)(2,1)}, u32[]{:S(2)}) copy-start(bf16[128,32,128]{2,1,0:T(8,128)(2,1)} %param.12) | copy-start | bytes 3145732
  1.9 6.2 %collective-permute-start.2 = (bf16[2,2,128,128]{3,2,1,0:T(8,128)(2,1)S(1)}, bf16[2,2,128,128]{3,2,1,0:T(8,128)(2,1)S(1)}, u32[]{:S(2)}, u32[]{:S(2)}) collective-permute-start(bf16[2,2,128,128]{3,2,1,0:T(8,128)(2,1)S(1)} %bitcast.67), channel_id=1, source_target_pairs={{0,1},{1,0},{2,3},{3,2},{4,5},{5,4},{6,7},{7,6},{8,9},{9,8},{10,11... | collective-permute-start | bytes 393224 | tf_op jit(solution)/shard_map/ppermute | solution.py:412
  5.6 1.5 copy-start
  5.6 2.0 %copy-start.11 = (s32[1,8]{1,0:T(1,128)S(1)}, s32[1,8]{1,0:T(1,128)}, u32[]{:S(2)}) copy-start(s32[1,8]{1,0:T(1,128)} %refs_0_.9) | copy-start | bytes 100
  5.7 17.9 %collective-permute-start = (bf16[16,128,128]{2,1,0:T(8,128)(2,1)S(1)}, bf16[16,128,128]{2,1,0:T(8,128)(2,1)S(1)}, u32[]{:S(2)}, u32[]{:S(2)}) collective-permute-start(bf16[16,128,128]{2,1,0:T(8,128)(2,1)S(1)} %dynamic-slice_bitcast_fusion.1), channel_id=1, source_target_pairs={{0,1},{1,0},{2,3},{3,2},{4,5},{5,4},{6,7},{7,6},{8,9},{9,8},{10,11... | collective-permute-start | bytes 1572872 | tf_op jit(solution)/shard_map/ppermute | solution.py:412
  6.2 26.2 %copy-start.1 = (bf16[32,128,128]{2,1,0:T(8,128)(2,1)}, bf16[32,128,128]{2,1,0:T(8,128)(2,1)S(1)}, u32[]{:S(2)}) copy-start(bf16[32,128,128]{2,1,0:T(8,128)(2,1)S(1)} %copy.50) | copy-start | bytes 3145732
  6.2 23.3 %copy-start.12 = (s32[16,8]{0,1:T(8,128)S(1)}, s32[16,8]{0,1:T(8,128)}, u32[]{:S(2)}) copy-start(s32[16,8]{0,1:T(8,128)} %param.16) | copy-start | bytes 1540
  6.2 24.0 %copy-start.13 = (s32[16,8]{0,1:T(8,128)S(1)}, s32[16,8]{0,1:T(8,128)}, u32[]{:S(2)}) copy-start(s32[16,8]{0,1:T(8,128)} %param.17) | copy-start | bytes 1540
  7.1 25.3 %collective-permute-start.1 = (bf16[16,128,128]{2,1,0:T(8,128)(2,1)}, bf16[16,128,128]{2,1,0:T(8,128)(2,1)}, u32[]{:S(2)}, u32[]{:S(2)}) collective-permute-start(bf16[16,128,128]{2,1,0:T(8,128)(2,1)} %dynamic-slice_bitcast_fusion), channel_id=1, source_target_pairs={{0,1},{1,0},{2,3},{3,2},{4,5},{5,4},{6,7},{7,6},{8,9},{9,8},{10,11... | collective-permute-start | bytes 1572872 | tf_op jit(solution)/shard_map/ppermute | solution.py:412
  8.1 24.3 %copy-start.2 = (bf16[2,2,2,128,128]{4,3,2,1,0:T(8,128)(2,1)}, bf16[2,2,2,128,128]{4,3,2,1,0:T(8,128)(2,1)S(1)}, u32[]{:S(2)}) copy-start(bf16[2,2,2,128,128]{4,3,2,1,0:T(8,128)(2,1)S(1)} %pad_maximum_fusion.3.refs_6_.refs_9_.kv) | copy-start | bytes 786436
  8.1 40.4 %collective-permute-start.6 = (bf16[2,2,2,128,128]{4,3,2,1,0:T(8,128)(2,1)S(1)}, bf16[2,2,2,128,128]{4,3,2,1,0:T(8,128)(2,1)}, u32[]{:S(2)}, u32[]{:S(2)}) collective-permute-start(bf16[2,2,2,128,128]{4,3,2,1,0:T(8,128)(2,1)S(1)} %pad_maximum_fusion.3.refs_6_.refs_9_.kv), channel_id=1, source_target_pairs={{0,8},{1,9},{2,10},{3,11},{4,12},{5,13},{6,14},{7,15},{16,24},{17,... | collective-permute-start | bytes 786440 | tf_op jit(solution)/shard_map/ppermute | solution.py:416
  11.9 36.6 %collective-permute-start.5 = (bf16[2,2,2,128,128]{4,3,2,1,0:T(8,128)(2,1)S(1)}, bf16[2,2,2,128,128]{4,3,2,1,0:T(8,128)(2,1)}, u32[]{:S(2)}, u32[]{:S(2)}) collective-permute-start(bf16[2,2,2,128,128]{4,3,2,1,0:T(8,128)(2,1)S(1)} %pad_maximum_fusion.3.refs_6_.refs_9_.kv), channel_id=1, source_target_pairs={{0,6},{1,7},{2,8},{3,9},{4,10},{5,11},{6,12},{7,13},{8,14},{9,15},... | collective-permute-start | bytes 786440 | tf_op jit(solution)/shard_map/ppermute | solution.py:416
  21.5 26.9 %collective-permute-start.4 = (bf16[2,2,2,128,128]{4,3,2,1,0:T(8,128)(2,1)S(1)}, bf16[2,2,2,128,128]{4,3,2,1,0:T(8,128)(2,1)}, u32[]{:S(2)}, u32[]{:S(2)}) collective-permute-start(bf16[2,2,2,128,128]{4,3,2,1,0:T(8,128)(2,1)S(1)} %pad_maximum_fusion.3.refs_6_.refs_9_.kv), channel_id=1, source_target_pairs={{0,4},{1,5},{2,6},{3,7},{4,8},{5,9},{6,10},{7,11},{8,12},{9,13},{1... | collective-permute-start | bytes 786440 | tf_op jit(solution)/shard_map/ppermute | solution.py:416
  23.5 0.8 copy-start.3
  24.4 24.1 %collective-permute-start.3 = (bf16[2,2,2,128,128]{4,3,2,1,0:T(8,128)(2,1)S(1)}, bf16[2,2,2,128,128]{4,3,2,1,0:T(8,128)(2,1)}, u32[]{:S(2)}, u32[]{:S(2)}) collective-permute-start(bf16[2,2,2,128,128]{4,3,2,1,0:T(8,128)(2,1)S(1)} %pad_maximum_fusion.3.refs_6_.refs_9_.kv), channel_id=1, source_target_pairs={{0,2},{1,3},{2,4},{3,5},{4,6},{5,7},{6,8},{7,9},{8,10},{9,11},{10,... | collective-permute-start | bytes 786440 | tf_op jit(solution)/shard_map/ppermute | solution.py:416
  57.9 8.4 %copy-start.15 = (s16[1040,128]{1,0:T(8,128)(2,1)S(1)}, s16[1040,128]{1,0:T(8,128)(2,1)}, u32[]{:S(2)}) copy-start(s16[1040,128]{1,0:T(8,128)(2,1)} %get-tuple-element.42) | copy-start | bytes 798724
  57.9 9.7 %copy-start.14 = (s16[1040,128]{1,0:T(8,128)(2,1)S(1)}, s16[1040,128]{1,0:T(8,128)(2,1)}, u32[]{:S(2)}) copy-start(s16[1040,128]{1,0:T(8,128)(2,1)} %get-tuple-element.43) | copy-start | bytes 798724
  63.7 84.0 %collective-permute-start.8 = (s16[1040,128]{1,0:T(8,128)(2,1)}, s16[1040,128]{1,0:T(8,128)(2,1)S(1)}, u32[]{:S(2)}, u32[]{:S(2)}) collective-permute-start(s16[1040,128]{1,0:T(8,128)(2,1)} %get-tuple-element.40), channel_id=1, source_target_pairs={{2,0},{3,1},{4,2},{5,3},{6,4},{7,5},{8,6},{9,7},{10,8},{11,9},{12,... | collective-permute-start | bytes 798728 | tf_op jit(solution)/shard_map/ppermute | solution.py:416
  65.0 82.7 %collective-permute-start.9 = (s16[1040,128]{1,0:T(8,128)(2,1)}, s16[1040,128]{1,0:T(8,128)(2,1)S(1)}, u32[]{:S(2)}, u32[]{:S(2)}) collective-permute-start(s16[1040,128]{1,0:T(8,128)(2,1)} %get-tuple-element.41), channel_id=1, source_target_pairs={{4,0},{5,1},{6,2},{7,3},{8,4},{9,5},{10,6},{11,7},{12,8},{13,9},{1... | collective-permute-start | bytes 798728 | tf_op jit(solution)/shard_map/ppermute | solution.py:416
  66.3 81.4 %collective-permute-start.10 = (s16[1040,128]{1,0:T(8,128)(2,1)S(1)}, s16[1040,128]{1,0:T(8,128)(2,1)S(1)}, u32[]{:S(2)}, u32[]{:S(2)}) collective-permute-start(s16[1040,128]{1,0:T(8,128)(2,1)S(1)} %copy-done.15), channel_id=1, source_target_pairs={{6,0},{7,1},{8,2},{9,3},{10,4},{11,5},{12,6},{13,7},{14,8},{15,9},... | collective-permute-start | bytes 798728 | tf_op jit(solution)/shard_map/ppermute | solution.py:416
  67.6 80.1 %collective-permute-start.11 = (s16[1040,128]{1,0:T(8,128)(2,1)S(1)}, s16[1040,128]{1,0:T(8,128)(2,1)S(1)}, u32[]{:S(2)}, u32[]{:S(2)}) collective-permute-start(s16[1040,128]{1,0:T(8,128)(2,1)S(1)} %copy-done.14), channel_id=1, source_target_pairs={{8,0},{9,1},{10,2},{11,3},{12,4},{13,5},{14,6},{15,7},{24,16},{25,... | collective-permute-start | bytes 798728 | tf_op jit(solution)/shard_map/ppermute | solution.py:416
  90.0 65.0 %copy-start.4 = (bf16[2,16,128,128]{3,2,1,0:T(8,128)(2,1)S(1)}, bf16[2,16,128,128]{3,2,1,0:T(8,128)(2,1)}, u32[]{:S(2)}) copy-start(bf16[2,16,128,128]{3,2,1,0:T(8,128)(2,1)} %get-tuple-element.37) | copy-start | bytes 3145732
  90.0 73.6 %all-to-all-start = ((f32[256,1,256]{2,1,0:T(1,128)}), f32[256,1,256]{2,1,0:T(1,128)S(1)}, u32[]{:S(2)}, u32[]{:S(2)}) async-start(f32[256,1,256]{2,1,0:T(1,128)} %broadcast_in_dim.50), calls=%async_computation | async-start | bytes 524288 | tf_op jit(solution)/shard_map/all_to_all | solution.py:471
  147.7 0.7 copy-start.7
  147.7 0.8 copy-start.8
  147.8 0.8 copy-start.9
  147.8 0.9 copy-start.10
  152.8 3.2 %collective-permute-start.12 = (bf16[2,2,128,128]{3,2,1,0:T(8,128)(2,1)S(1)}, bf16[2,2,128,128]{3,2,1,0:T(8,128)(2,1)S(1)}, u32[]{:S(2)}, u32[]{:S(2)}) collective-permute-start(bf16[2,2,128,128]{3,2,1,0:T(8,128)(2,1)S(1)} %slice_bitcast_fusion.3), channel_id=1, source_target_pairs={{0,1},{1,0},{2,3},{3,2},{4,5},{5,4},{6,7},{7,6},{8,9},{9,8},{10,11... | collective-permute-start | bytes 393224 | tf_op jit(solution)/shard_map/ppermute | solution.py:412
  155.0 9.3 %collective-permute-start.7 = (bf16[16,128,128]{2,1,0:T(8,128)(2,1)S(1)}, bf16[16,128,128]{2,1,0:T(8,128)(2,1)S(1)}, u32[]{:S(2)}, u32[]{:S(2)}) collective-permute-start(bf16[16,128,128]{2,1,0:T(8,128)(2,1)S(1)} %slice_bitcast_fusion), channel_id=1, source_target_pairs={{0,1},{1,0},{2,3},{3,2},{4,5},{5,4},{6,7},{7,6},{8,9},{9,8},{10,11... | collective-permute-start | bytes 1572872 | tf_op jit(solution)/shard_map/ppermute | solution.py:412

commit v2 on v1

v2 whole, which is shorter than its diff:
```python
import functools
import math

import jax
import jax.numpy as jnp
from jax import lax
from jax.experimental import pallas as pl
from jax.experimental.pallas import tpu as pltpu
from jax.sharding import PartitionSpec as P

EPS = 1e-06
TOK = 128
HD = 128
BLK = 2 * TOK
REACH = 4
GROUP = 8
HEADS = 2
SLOTS = HEADS * 2 * (GROUP // 2)
ROOT = 1.0 / math.sqrt(HD)
EXP_SCALE = ROOT * math.log2(math.e)
MASKED = -1e30
UNROLL = 4
QMAX = 32000.0
GAP_MAX = 64.0 / EXP_SCALE
VMEM = pltpu.CompilerParams(vmem_limit_bytes=56 * 1024 * 1024)

f32, bf16, i32 = jnp.float32, jnp.bfloat16, jnp.int32


def dot(a, b, dims):
    return lax.dot_general(a, b, (dims, ((), ())), preferred_element_type=f32)


def inv_rms(x):
    return lax.rsqrt(jnp.mean(x * x, axis=-1, keepdims=True) + EPS)


def turn(x):
    return pltpu.roll(x, HD // 2, x.ndim - 1)


def tables(cs):
    other = turn(cs)
    low = lax.broadcasted_iota(i32, cs.shape, cs.ndim - 1) < HD // 2
    return jnp.where(low, cs, other), jnp.where(low, -other, cs)


def norm_rope(x, gain, cosine, sine):
    xn = x * inv_rms(x) * gain
    return xn * cosine + turn(xn) * sine


def unrotate(x, gain, cosine, sine, incoming):
    dn = incoming * cosine - turn(incoming) * sine
    r = inv_rms(x)
    unit = x * r
    u = dn * gain
    grad = r * (u - unit * jnp.mean(u * unit, axis=-1, keepdims=True))
    return grad, jnp.sum(dn * unit, axis=0, keepdims=True)


def token_base(place, k, half):
    chip, core = place // 2, place % 2
    return ((chip - k) * 2 + jnp.where(half == 0, core, 1 - core)) * TOK


def fill_bias(bias, blocks, half, lens):
    place = lax.axis_index("ctx")
    qidx = token_base(place, 0, half) + lax.broadcasted_iota(i32, (1, TOK), 1)
    start, total = jnp.zeros_like(qidx), jnp.int32(0)
    for j in range(lens.shape[1]):
        total = total + lens[0, j]
        start = jnp.where(qidx >= total, total, start)
    for n, k in enumerate(blocks):
        for part in range(2):
            kidx = token_base(place, k, part) + lax.broadcasted_iota(i32, (TOK, TOK), 0)
            good = (kidx <= qidx) & (kidx >= start)
            at = n * BLK + part * TOK
            bias[half, at : at + TOK, :] = jnp.where(good, 0.0, MASKED)


def load_block(n, k, kv, cs, gain_row, kr, vv):
    for part in range(2):
        rows = slice(part * TOK, (part + 1) * TOK)
        at = n * BLK + part * TOK
        cosine, sine = tables(cs[k, rows, :])
        x = kv[part, 0, 0].astype(f32)
        kr[at : at + TOK, :] = norm_rope(x, gain_row, cosine, sine).astype(bf16)
        vv[at : at + TOK, :] = kv[part, 1, 0]


def widen(ref, rows):
    half = ref[rows, :]
    return jnp.concatenate([half, half], axis=1)


def prep_kernel(
    lens, ids, grades, q_own, q_other, g_own, g_other, q_gain, k_gain, cs, kv,
    q_out, g_out, m_out, l_out, d_out, kr_out, kr, vv, bias, weights,
):
    head, half = pl.program_id(0), pl.program_id(1)
    place, row = lax.axis_index("ctx"), lax.axis_index("dp")

    @pl.when((half == 0) & (head == 0))
    def _():
        adv = []
        pid, grd = ids[...].astype(f32), grades[...].astype(f32)
        at_row = lax.broadcasted_iota(i32, pid.shape, 0) == row
        at_col = lax.broadcasted_iota(i32, pid.shape, 1)
        for j in range(lens.shape[1]):
            at = at_row & (at_col == j)
            name = jnp.sum(jnp.where(at, pid, 0.0), keepdims=True)
            own = jnp.sum(jnp.where(at, grd, 0.0), keepdims=True)
            same = jnp.where(pid == name, 1.0, 0.0)
            count = jnp.sum(same, keepdims=True)
            centre = jnp.sum(same * grd, keepdims=True) / count
            spread = grd - centre
            variance = jnp.sum(same * spread * spread, keepdims=True) / count
            adv.append((own - centre) / jnp.maximum(jnp.sqrt(variance), 1.0))
        for part in range(2):
            idx = token_base(place, 0, part) + lax.broadcasted_iota(i32, (TOK, HD), 0)
            weight = jnp.zeros((TOK, HD), f32)
            total = jnp.int32(0)
            for j in range(lens.shape[1]):
                weight = jnp.where(idx >= total, adv[j], weight)
                total = total + lens[0, j]
            weights[part] = weight
            fill_bias(bias, (0,), part, lens)

    @pl.when(half == 0)
    def _():
        load_block(0, 0, kv, cs, k_gain[...], kr, vv)
        kr_out[0] = kr[...]

    rows = pl.ds(pl.multiple_of(half * TOK, TOK), TOK)
    cosine, sine = tables(cs[0, rows, :])
    first = half == 0

    def body(two, carry):
        for e in range(2):
            n = two * 2 + e
            x = jnp.where(first, q_own[n], q_other[n]).astype(f32)
            g = jnp.where(first, g_own[n], g_other[n]).astype(f32)
            at = slice(e * TOK, (e + 1) * TOK)
            q_out[two, at, :] = norm_rope(x, q_gain[...], cosine, sine).astype(bf16)
            g_out[two, at, :] = (weights[half] * g).astype(bf16)
        s = dot(kr[...], q_out[two], ((1,), (1,))) + widen(bias.at[half], slice(None))
        dp = dot(vv[...], g_out[two], ((1,), (1,)))
        m = jnp.max(s, axis=0, keepdims=True)
        e = jnp.exp2((s - m) * EXP_SCALE)
        m_out[two] = m
        l_out[two] = jnp.sum(e, axis=0, keepdims=True)
        d_out[two] = jnp.sum(e * dp, axis=0, keepdims=True)
        return carry

    lax.fori_loop(0, GROUP // 2, body, 0, unroll=UNROLL)


def gain_term(k, n, kv, cs, dk):
    total = jnp.zeros((1, HD), f32)
    for part in range(2):
        rows = slice(part * TOK, (part + 1) * TOK)
        at = n * BLK + part * TOK
        cosine, sine = tables(cs[k, rows, :])
        x = kv[part, 0, 0].astype(f32)
        incoming = dk[at : at + TOK, :]
        dn = incoming * cosine - turn(incoming) * sine
        total = total + jnp.sum(dn * (x * inv_rms(x)), axis=0, keepdims=True)
    return total * ROOT


def code(n, head, dk, dv, packed):
    marks = packed[2 * HEADS * BLK :, :].astype(i32).astype(f32)
    rows = lax.broadcasted_iota(i32, (16, HD), 0)
    for kind, ref in enumerate((dk, dv)):
        x = ref[n * BLK : (n + 1) * BLK, :]
        peak = jnp.maximum(jnp.max(jnp.abs(x), axis=0, keepdims=True), 1e-30)
        mark = jnp.ceil(jnp.log2(peak) * 256.0)
        marks = jnp.where(rows == kind * HEADS + head, mark, marks)
        fixed = x * (jnp.exp2(mark * (-1.0 / 256.0)) * QMAX)
        at = pl.multiple_of((kind * HEADS + head) * BLK, BLK)
        packed[pl.ds(at, BLK), :] = jnp.floor(fixed + 0.5).astype(i32).astype(jnp.int16)
    packed[2 * HEADS * BLK :, :] = marks.astype(i32).astype(jnp.int16)


FAR = (4, 3, 2, 1)
NEAR = (2, 1, 0)


def far_kernel(
    lens, k_gain, cs, q, g, m_in, l_in, d_in, kv4, kv3, kv2, kv1,
    dq, lse_out, mean_out, terms, pack4, pack3, kr_out, kr, vv, krt, bias, dk, dv,
):
    head, half = pl.program_id(0), pl.program_id(1)
    kvs, packs = (kv4, kv3, kv2, kv1), (pack4, pack3)
    done = len(packs) * BLK
    place = lax.axis_index("ctx")
    base, total, opening = token_base(place, 0, half), jnp.int32(0), jnp.int32(0)
    for j in range(lens.shape[1]):
        total = total + lens[0, j]
        opening = jnp.where(base >= total, total, opening)
    reaches = opening < (place // 2) * BLK

    @pl.when((head == 0) & (half == 0))
    def _():
        terms[...] = jnp.zeros(terms.shape, f32)
        for pack in packs:
            pack[2 * HEADS * BLK :, :] = jnp.zeros((16, HD), jnp.int16)
        for part in range(2):
            fill_bias(bias, FAR, part, lens)

    @pl.when(half == 0)
    def _():
        for n, k in enumerate(FAR):
            load_block(n, k, kvs[n], cs, k_gain[...], kr, vv)
        krt[...] = jnp.transpose(kr[:done, :].astype(f32)).astype(bf16)
        kr_out[0] = kr[done:, :]

    dk[half] = jnp.zeros(dk.shape[1:], f32)
    dv[half] = jnp.zeros(dv.shape[1:], f32)

    def finish(two, e, dp, m, l, d):
        mean = d / l
        lse_out[two] = m * EXP_SCALE + jnp.log2(l)
        mean_out[two] = mean
        p = e[:done] * (1.0 / l)
        ds = (p * (dp[:done] - mean)).astype(bf16)
        dv[half] += dot(p.astype(bf16), g[two], ((1,), (0,)))
        dk[half] += dot(ds, q[two], ((1,), (0,)))
        dq[two] = dot(krt[...], ds, ((1,), (0,)))

    def products(two):
        s = dot(kr[...], q[two], ((1,), (1,))) + widen(bias.at[half], slice(None))
        return s, dot(vv[...], g[two], ((1,), (1,)))

    def near_peak(two, above):
        s, dp = products(two)
        m = m_in[two]
        gap = s - m
        e = jnp.exp2(gap * EXP_SCALE)
        l = l_in[two] + jnp.sum(e, axis=0, keepdims=True)
        d = d_in[two] + jnp.sum(e * dp, axis=0, keepdims=True)
        finish(two, e, dp, m, l, d)
        return jnp.maximum(above, jnp.max(gap, axis=0, keepdims=True))

    def any_peak(two, carry):
        s, dp = products(two)
        m_old = m_in[two]
        m = jnp.maximum(m_old, jnp.max(s, axis=0, keepdims=True))
        e = jnp.exp2((s - m) * EXP_SCALE)
        fade = jnp.exp2((m_old - m) * EXP_SCALE)
        l = l_in[two] * fade + jnp.sum(e, axis=0, keepdims=True)
        d = d_in[two] * fade + jnp.sum(e * dp, axis=0, keepdims=True)
        finish(two, e, dp, m, l, d)
        return carry

    @pl.when(reaches)
    def _():
        start = jnp.full((1, BLK), MASKED, f32)
        above = lax.fori_loop(0, GROUP // 2, near_peak, start, unroll=UNROLL)

        @pl.when(jnp.max(above) > GAP_MAX)
        def _():
            dk[half] = jnp.zeros(dk.shape[1:], f32)
            dv[half] = jnp.zeros(dv.shape[1:], f32)
            lax.fori_loop(0, GROUP // 2, any_peak, 0)

    @pl.when(jnp.logical_not(reaches))
    def _():
        lse_out[...] = m_in[...] * EXP_SCALE + jnp.log2(l_in[...])
        mean_out[...] = d_in[...] / l_in[...]
        dq[...] = jnp.zeros(dq.shape, f32)

    @pl.when(half == 1)
    def _():
        dk[0] += dk[1]
        dv[0] += dv[1]
        for n, k in enumerate(FAR[: len(packs)]):
            terms[1:2, :] = terms[1:2, :] + gain_term(k, n, kvs[n], cs, dk.at[0])
            code(n, head, dk.at[0], dv.at[0], packs[n])


def near_kernel(
    lens, q_gain, cs, q, g, lse, mean, dq_in, terms_in, q_own, q_other, kr21, kr0, kv2, kv1, kv0,
    q_grad, terms, pack2, pack1, dk_own, dv_own, kr, vv, krt, bias, dk, dv,
):
    head, half = pl.program_id(0), pl.program_id(1)
    kvs, packs = (kv2, kv1, kv0), (pack2, pack1)

    @pl.when((head == 0) & (half == 0))
    def _():
        terms[...] = terms_in[...]
        for pack in packs:
            pack[2 * HEADS * BLK :, :] = jnp.zeros((16, HD), jnp.int16)
        for part in range(2):
            fill_bias(bias, NEAR, part, lens)

    @pl.when(half == 0)
    def _():
        kr[: 2 * BLK, :] = kr21[0]
        kr[2 * BLK :, :] = kr0[0]
        for n in range(len(NEAR)):
            for part in range(2):
                at = n * BLK + part * TOK
                vv[at : at + TOK, :] = kvs[n][part, 1, 0]
        krt[...] = jnp.transpose(kr[...].astype(f32)).astype(bf16)
        dk[...] = jnp.zeros(dk.shape, f32)
        dv[...] = jnp.zeros(dv.shape, f32)

    rows = pl.ds(pl.multiple_of(half * TOK, TOK), TOK)
    cosine, sine = tables(cs[0, rows, :])
    first = half == 0

    def body(two, total):
        s = dot(kr[...], q[two], ((1,), (1,))) + widen(bias.at[half], slice(None))
        dp = dot(vv[...], g[two], ((1,), (1,)))
        p = jnp.exp2(s * EXP_SCALE - lse[two])
        ds = (p * (dp - mean[two])).astype(bf16)
        dv[...] += dot(p.astype(bf16), g[two], ((1,), (0,)))
        dk[...] += dot(ds, q[two], ((1,), (0,)))
        incoming = jnp.transpose(dq_in[two] + dot(krt[...], ds, ((1,), (0,)))) * ROOT
        for e in range(2):
            n = two * 2 + e
            x = jnp.where(first, q_own[n], q_other[n]).astype(f32)
            grad, part = unrotate(
                x, q_gain[...], cosine, sine, incoming[e * TOK : (e + 1) * TOK, :]
            )
            q_grad[0, n] = grad.astype(bf16)
            total = total + part
        return total

    total = lax.fori_loop(0, GROUP // 2, body, jnp.zeros((1, HD), f32), unroll=UNROLL)
    terms[0:1, :] = terms[0:1, :] + total

    @pl.when(half == 1)
    def _():
        for n, k in enumerate(NEAR):
            terms[1:2, :] = terms[1:2, :] + gain_term(k, n, kvs[n], cs, dk)
            if k > 0:
                code(n, head, dk, dv, packs[n])
            else:
                dk_own[0] = dk[n * BLK : (n + 1) * BLK, :]
                dv_own[0] = dv[n * BLK : (n + 1) * BLK, :]


def finish_kernel(gain, cs, kv, dk, dv, p1, p2, p3, p4, mine, other):
    gain_row = gain[...]
    packs, outs = (p1, p2, p3, p4), (mine, other)
    marks = [p[2 * HEADS * BLK :, :].astype(i32).astype(f32) for p in packs]
    for kind, ref in enumerate((dk, dv)):
        for head in range(HEADS):
            n = kind * HEADS + head
            scales = [jnp.exp2(k[n : n + 1, :] * (1.0 / 256.0)) * (1.0 / QMAX) for k in marks]
            for half in range(2):
                rows = slice(half * TOK, (half + 1) * TOK)
                total = ref[head, rows, :]
                for p, scale in zip(packs, scales):
                    at = n * BLK + half * TOK
                    total = total + p[at : at + TOK, :].astype(i32).astype(f32) * scale
                if kind == 0:
                    x = kv[half, 0, head].astype(f32)
                    cosine, sine = tables(cs[0, rows, :])
                    total, _ = unrotate(x, gain_row, cosine, sine, total * ROOT)
                outs[half][kind, head] = total.astype(bf16)


def vmem(count):
    return [pl.BlockSpec(memory_space=pltpu.VMEM)] * count


def smem(count):
    return [pl.BlockSpec(memory_space=pltpu.SMEM)] * count


def spec(shape, index):
    return pl.BlockSpec(shape, index)


PAIRS = GROUP // 2
Q_BLOCK = (PAIRS, BLK, HD)
STAT_BLOCK = (PAIRS, 1, BLK)
DQ_BLOCK = (PAIRS, HD, BLK)
RAW_BLOCK = (GROUP, TOK, HD)
KV_BLOCK = (2, 2, 1, TOK, HD)
STAT = jax.ShapeDtypeStruct((SLOTS, 1, BLK), f32)
TERMS = jax.ShapeDtypeStruct((8, HD), f32)
PACK = jax.ShapeDtypeStruct((2 * HEADS * BLK + 16, HD), jnp.int16)
OWN = jax.ShapeDtypeStruct((HEADS, BLK, HD), f32)


def by_slot(head, half):
    return (head * 2 + half, 0, 0)


def by_head(head, half):
    return (head, 0, 0)


def kv_at(head, half):
    return (0, 0, head, 0, 0)


def whole(ndim):
    return lambda head, half: (0,) * ndim


def own_raw(head, half):
    return (head, 0, 0)


def block_scratch(done, blocks):
    return [
        pltpu.VMEM((blocks * BLK, HD), bf16),
        pltpu.VMEM((blocks * BLK, HD), bf16),
        pltpu.VMEM((HD, done * BLK), bf16),
        pltpu.VMEM((2, blocks * BLK, TOK), f32),
        pltpu.VMEM((done * BLK, HD), f32),
        pltpu.VMEM((done * BLK, HD), f32),
    ]


def prepare(lengths, ids, grades, q_own, q_other, g_own, g_other, q_gain, k_gain, cs, kv):
    rows = jax.ShapeDtypeStruct((SLOTS, BLK, HD), bf16)
    return pl.pallas_call(
        prep_kernel,
        grid=(HEADS, 2),
        out_shape=[rows, rows, STAT, STAT, STAT, jax.ShapeDtypeStruct((HEADS, BLK, HD), bf16)],
        in_specs=smem(1)
        + [spec(ids.shape, whole(2))] * 2
        + [spec(RAW_BLOCK, own_raw)] * 4
        + [spec((1, HD), whole(2))] * 2
        + [spec((1, BLK, HD), whole(3)), spec(KV_BLOCK, kv_at)],
        out_specs=[spec(Q_BLOCK, by_slot)] * 2
        + [spec(STAT_BLOCK, by_slot)] * 3
        + [spec((1, BLK, HD), by_head)],
        scratch_shapes=[
            pltpu.VMEM((BLK, HD), bf16),
            pltpu.VMEM((BLK, HD), bf16),
            pltpu.VMEM((2, BLK, TOK), f32),
            pltpu.VMEM((2, TOK, HD), f32),
        ],
        compiler_params=VMEM,
        name="prepare",
    )(lengths, ids, grades, q_own, q_other, g_own, g_other, q_gain, k_gain, cs, kv)


def far(lengths, k_gain, cs, q, g, stats, kvs):
    dq = jax.ShapeDtypeStruct((SLOTS, HD, BLK), f32)
    near_keys = jax.ShapeDtypeStruct((HEADS, 2 * BLK, HD), bf16)
    return pl.pallas_call(
        far_kernel,
        grid=(HEADS, 2),
        out_shape=[dq, STAT, STAT, TERMS, PACK, PACK, near_keys],
        in_specs=smem(1)
        + [spec((1, HD), whole(2)), spec(cs.shape, whole(3))]
        + [spec(Q_BLOCK, by_slot)] * 2
        + [spec(STAT_BLOCK, by_slot)] * 3
        + [spec(KV_BLOCK, kv_at)] * 4,
        out_specs=[spec(DQ_BLOCK, by_slot), spec(STAT_BLOCK, by_slot), spec(STAT_BLOCK, by_slot)]
        + [spec(TERMS.shape, whole(2))]
        + [spec(PACK.shape, whole(2))] * 2
        + [spec((1, 2 * BLK, HD), by_head)],
        scratch_shapes=block_scratch(2, 4)[:4] + [pltpu.VMEM((2, 2 * BLK, HD), f32)] * 2,
        compiler_params=VMEM,
        name="far",
    )(lengths, k_gain, cs, q, g, *stats, *kvs)


def near(lengths, q_gain, cs, q, g, lse, mean, dq, terms, q_own, q_other, kr21, kr0, kvs):
    row = spec((1, HD), whole(2))
    return pl.pallas_call(
        near_kernel,
        grid=(HEADS, 2),
        out_shape=[
            jax.ShapeDtypeStruct((2, HEADS * GROUP, TOK, HD), bf16),
            TERMS, PACK, PACK, OWN, OWN,
        ],
        in_specs=smem(1)
        + [row, spec((3, BLK, HD), whole(3))]
        + [spec(Q_BLOCK, by_slot)] * 2
        + [spec(STAT_BLOCK, by_slot)] * 2
        + [spec(DQ_BLOCK, by_slot), spec(TERMS.shape, whole(2))]
        + [spec(RAW_BLOCK, own_raw)] * 2
        + [spec((1, 2 * BLK, HD), by_head), spec((1, BLK, HD), by_head)]
        + [spec(KV_BLOCK, kv_at)] * 3,
        out_specs=[spec((1,) + RAW_BLOCK, lambda head, half: (half, head, 0, 0))]
        + [spec(TERMS.shape, whole(2))]
        + [spec(PACK.shape, whole(2))] * 2
        + [spec((1, BLK, HD), by_head)] * 2,
        scratch_shapes=block_scratch(3, 3),
        compiler_params=VMEM,
        name="near",
    )(lengths, q_gain, cs, q, g, lse, mean, dq, terms, q_own, q_other, kr21, kr0, *kvs)


def rope_tables(place, lens):
    chip, core = place // 2, place % 2
    k = jnp.arange(REACH + 1, dtype=i32)[:, None, None]
    half = jnp.arange(2, dtype=i32)[None, :, None]
    t = jnp.arange(TOK, dtype=i32)[None, None, :]
    index = (((chip - k) * 2 + jnp.where(half == 0, core, 1 - core)) * TOK + t).reshape(
        REACH + 1, BLK
    )
    tri = jnp.arange(lens.shape[1])
    ends = jnp.sum(jnp.where(tri[None, :] <= tri[:, None], lens[0][None, :], 0), axis=1)
    start = jnp.max(jnp.where(index[..., None] >= ends, ends, 0), axis=-1)
    freqs = jnp.power(1000000.0, -(jnp.arange(HD // 2, dtype=f32) * (2.0 / HD)))
    angles = (index - start).astype(f32)[..., None] * freqs
    return jnp.concatenate([jnp.cos(angles), jnp.sin(angles)], axis=-1)


def swap_cores(x):
    return lax.ppermute(x, "ctx", [(i, i ^ 1) for i in range(16)])


def shift_chips(x, k):
    return lax.ppermute(x, "ctx", [(i, i + 2 * k) for i in range(16) if 0 <= i + 2 * k < 16])


def on_device(queries, keys, values, out_grad, q_gain, k_gain, lengths, prompt_ids, grades):
    place = lax.axis_index("ctx")
    core = place % 2
    q_gain2, k_gain2 = q_gain.reshape(1, HD), k_gain.reshape(1, HD)

    kv = jnp.stack([keys, values]).transpose(2, 0, 1, 3).reshape(2, HEADS, 2, TOK, HD)
    kv = kv.transpose(0, 2, 1, 3, 4)
    kv_mine = lax.dynamic_index_in_dim(kv, core, 0, keepdims=False)
    kv_other = swap_cores(lax.dynamic_index_in_dim(kv, 1 - core, 0, keepdims=False))
    own = jnp.stack([kv_mine, kv_other])
    blocks = [own] + [shift_chips(own, k) for k in range(1, REACH + 1)]

    heads = HEADS * GROUP
    q_t = queries.transpose(1, 0, 2).reshape(2, heads, TOK, HD)
    g_t = out_grad.transpose(1, 0, 2).reshape(2, heads, TOK, HD)
    q_own = lax.dynamic_index_in_dim(q_t, core, 0, keepdims=False)
    g_own = lax.dynamic_index_in_dim(g_t, core, 0, keepdims=False)
    q_other = swap_cores(lax.dynamic_index_in_dim(q_t, 1 - core, 0, keepdims=False))
    g_other = swap_cores(lax.dynamic_index_in_dim(g_t, 1 - core, 0, keepdims=False))
    cs = rope_tables(place, lengths)

    q, g, m, l, d, kr0 = prepare(
        lengths, prompt_ids, grades, q_own, q_other, g_own, g_other, q_gain2, k_gain2, cs, own
    )
    dq, lse, mean, terms, pack4, pack3, kr21 = far(
        lengths, k_gain2, cs, q, g, (m, l, d), [blocks[k] for k in FAR]
    )
    back4, back3 = shift_chips(pack4, -4), shift_chips(pack3, -3)
    q_half, terms, pack2, pack1, dk, dv = near(
        lengths, q_gain2, cs, q, g, lse, mean, dq, terms, q_own, q_other, kr21, kr0,
        [blocks[k] for k in NEAR],
    )
    back2, back1 = shift_chips(pack2, -2), shift_chips(pack1, -1)

    q_swapped = swap_cores(q_half[1])
    first = jnp.where(core == 0, q_half[0], q_swapped)
    second = jnp.where(core == 0, q_swapped, q_half[0])
    q_grad = jnp.concatenate([first, second]).transpose(1, 0, 2)

    pair = terms[:2].reshape(1, 2 * HD)
    pair, back4, back3 = lax.optimization_barrier((pair, back4, back3))
    count = lax.axis_size("dp") * lax.axis_size("ctx")
    gathered = lax.all_to_all(
        jnp.broadcast_to(pair, (count, 2 * HD)), ("dp", "ctx"), 0, 0, tiled=True
    )
    gains = jnp.sum(gathered, axis=0)

    mine, other = pl.pallas_call(
        finish_kernel,
        out_shape=[jax.ShapeDtypeStruct((2, HEADS, TOK, HD), bf16)] * 2,
        in_specs=vmem(9),
        out_specs=vmem(2),
        compiler_params=VMEM,
        name="finish",
    )(k_gain2, cs, own, dk, dv, back1, back2, back3, back4)
    other = swap_cores(other)
    first = jnp.where(core == 0, mine, other)
    second = jnp.where(core == 0, other, mine)
    kv_grad = jnp.concatenate([first, second], axis=1).transpose(0, 2, 1, 3)
    return (q_grad, kv_grad[0], kv_grad[1], gains[:HD], gains[HD:])


def solution(mesh):
    rows = P(("dp", "ctx"), None, None)
    return jax.shard_map(
        on_device,
        mesh=mesh,
        in_specs=(rows, rows, rows, rows, P(), P(), P("dp", None), P(), P()),
        out_specs=(rows, rows, rows, P(), P()),
        check_vma=False,
    )
```

time: 167 us -> 149 us (0.89)
  starting transfers between devices: 87.4 us -> 59.9 us
  waiting for transfers between devices: 5.92 us -> 32.3 us
  Pallas kernels: 53.9 us -> 34.7 us
  local copies, waits for them, and re-layouts: 12.3 us -> 14.8 us
    all_to_all x1, starting transfers between devices: 57.7 us -> 27.1 us  [on_device(): lax.all_to_all(jnp.broadcast_to(pair, (count, 2 * HD)), ('dp', 'ctx'), 0,...]
    ppermute x8, waiting for transfers between devices: 0.02 us -> 20.8 us  [shift_chips(): lax.ppermute(x, 'ctx', [(i, i + 2 * k) for i in range(16) if 0 <= i + 2 *...]
    pallas_call x7 -> x4, Pallas kernels: 53.9 us -> 34.7 us  [the longest x1 14.3 us: near(): pl.pallas_call(near_kernel, grid=(HEADS, 2), out_shape=[jax.ShapeDtypeStr...]
    all_to_all x1, waiting for transfers between devices: 5.07 us -> 11.5 us  [on_device(): lax.all_to_all(jnp.broadcast_to(pair, (count, 2 * HD)), ('dp', 'ctx'), 0,...]
    ppermute x5, starting transfers between devices: 6.29 us -> 10.3 us  [swap_cores(): return lax.ppermute(x, 'ctx', [(i, i ^ 1) for i in range(16)])]
    unnamed x40 -> x42, local copies, waits for them, and re-layouts: 6.4 us -> 9.99 us
    neg x1 -> x0, other arithmetic: 2.35 us -> none  [rope_tables(): -sine]
    cos x0 -> x1, other arithmetic: none -> 2.33 us  [rope_tables(): return jnp.concatenate([jnp.cos(angles), jnp.sin(angles)], axis=-1)]
  transfers between devices with their start and end apart: 14 -> 14, of which waited for: 2 -> 4; matrix products, arithmetic and copies ran while one was open for 8% -> 10% of each run, Pallas kernels for 23% -> 16%
where the time goes in v2:
time: 149 us; the launch traced here: 148 us
  starting transfers between devices  59.9 us (40%)
  Pallas kernels  34.7 us (23%)
  waiting for transfers between devices  32.3 us (22%)
  local copies, waits for them, and re-layouts  14.8 us (10%)
  other arithmetic  5.19 us (3%)
    all_to_all x1, starting transfers between devices, on_device(): lax.all_to_all(jnp.broadcast_to(pair, (count, 2 * HD)), ('dp', 'ctx'), 0,...  27.1 us
    ppermute x8, starting transfers between devices, shift_chips(): lax.ppermute(x, 'ctx', [(i, i + 2 * k) for i in range(16) if 0 <= i + 2 *...  22.5 us
    ppermute x8, waiting for transfers between devices, shift_chips(): lax.ppermute(x, 'ctx', [(i, i + 2 * k) for i in range(16) if 0 <= i + 2 *...  20.8 us
    pallas_call x1, Pallas kernels, near(): pl.pallas_call(near_kernel, grid=(HEADS, 2), out_shape=[jax.ShapeDtypeStr...  14.3 us
    all_to_all x1, waiting for transfers between devices, on_device(): lax.all_to_all(jnp.broadcast_to(pair, (count, 2 * HD)), ('dp', 'ctx'), 0,...  11.5 us
    ppermute x5, starting transfers between devices, swap_cores(): return lax.ppermute(x, 'ctx', [(i, i ^ 1) for i in range(16)])  10.3 us
    unnamed x42, local copies, waits for them, and re-layouts  9.99 us
    pallas_call x1, Pallas kernels, prepare(): pl.pallas_call(prep_kernel, grid=(HEADS, 2), out_shape=[rows, rows, STAT,...  9.86 us
  transfers between devices with their start and end apart: 14, of which 4 were waited for; matrix products, arithmetic and copies ran while one was open for 10% of the time, Pallas kernels for 16%

profile of v2, /device:TPU:1, one launch (start us, length us, event | category | flops | bytes accessed | tf_op | source)
XLA Modules:
  0.0 147.9 jit_solution(11330582665780211725)
XLA Ops:
  0.7 1.1 copy_bitcast_fusion.6
  1.8 3.3 %collective-permute-start.2 = (bf16[2,2,128,128]{3,2,1,0:T(8,128)(2,1)S(1)}, bf16[2,2,128,128]{3,2,1,0:T(8,128)(2,1)S(1)}, u32[]{:S(2)}, u32[]{:S(2)}) collective-permute-start(bf16[2,2,128,128]{3,2,1,0:T(8,128)(2,1)S(1)} %bitcast.69), channel_id=1, source_target_pairs={{0,1},{1,0},{2,3},{3,2},{4,5},{5,4},{6,7},{7,6},{8,9},{9,8},{10,11... | collective-permute-start | bytes 393224 | tf_op jit(solution)/shard_map/ppermute | solution.py:513
  5.2 1.6 %constant_dynamic-slice_fusion.1 = (bf16[1,16,128,128]{3,1,0,2:T(8,128)(2,1)S(1)}, bf16[1,16,128,128]{3,1,0,2:T(8,128)(2,1)S(1)}, bf16[1,16,128,128]{3,1,0,2:T(8,128)(2,1)S(1)}, bf16[1,16,128,128]{3,1,0,2:T(8,128)(2,1)S(1)}) fusion(bf16[2,16,128,128]{3,1,0,2:T(8,128)(2,1)S(1)} %bitcast.63, s32[]{:T(128)S(6)} %select_n.73, s32[]{:T(128)S(6)} %select_n.72, ...), kind=kLoop, calls=%fused_computation.31 | loop fusion | bytes 4194312 | tf_op jit(solution)/shard_map/jit(dynamic_index_in_dim)/dynamic_slice | solution.py:538
  8.9 1.4 copy.58.grades
  10.2 0.9 copy.85
  11.2 1.0 copy.87
  12.2 7.1 %collective-permute-start.6 = (bf16[2,2,2,128,128]{4,3,2,1,0:T(8,128)(2,1)S(1)}, bf16[2,2,2,128,128]{4,3,2,1,0:T(8,128)(2,1)S(1)}, u32[]{:S(2)}, u32[]{:S(2)}) collective-permute-start(bf16[2,2,2,128,128]{4,3,2,1,0:T(8,128)(2,1)S(1)} %pad_maximum_fusion.2.kv.kv0), channel_id=1, source_target_pairs={{0,2},{1,3},{2,4},{3,5},{4,6},{5,7},{6,8},{7,9},{8,10},{9,11},{10,... | collective-permute-start | bytes 786440 | tf_op jit(solution)/shard_map/ppermute | solution.py:517
  19.3 3.2 %collective-permute-start.5 = (bf16[2,2,2,128,128]{4,3,2,1,0:T(8,128)(2,1)S(1)}, bf16[2,2,2,128,128]{4,3,2,1,0:T(8,128)(2,1)S(1)}, u32[]{:S(2)}, u32[]{:S(2)}) collective-permute-start(bf16[2,2,2,128,128]{4,3,2,1,0:T(8,128)(2,1)S(1)} %pad_maximum_fusion.2.kv.kv0), channel_id=1, source_target_pairs={{0,4},{1,5},{2,6},{3,7},{4,8},{5,9},{6,10},{7,11},{8,12},{9,13},{1... | collective-permute-start | bytes 786440 | tf_op jit(solution)/shard_map/ppermute | solution.py:517
  22.5 2.9 %collective-permute-start.4 = (bf16[2,2,2,128,128]{4,3,2,1,0:T(8,128)(2,1)S(1)}, bf16[2,2,2,128,128]{4,3,2,1,0:T(8,128)(2,1)S(1)}, u32[]{:S(2)}, u32[]{:S(2)}) collective-permute-start(bf16[2,2,2,128,128]{4,3,2,1,0:T(8,128)(2,1)S(1)} %pad_maximum_fusion.2.kv.kv0), channel_id=1, source_target_pairs={{0,6},{1,7},{2,8},{3,9},{4,10},{5,11},{6,12},{7,13},{8,14},{9,15},... | collective-permute-start | bytes 786440 | tf_op jit(solution)/shard_map/ppermute | solution.py:517
  25.4 3.7 %collective-permute-start.3 = (bf16[2,2,2,128,128]{4,3,2,1,0:T(8,128)(2,1)S(1)}, bf16[2,2,2,128,128]{4,3,2,1,0:T(8,128)(2,1)S(1)}, u32[]{:S(2)}, u32[]{:S(2)}) collective-permute-start(bf16[2,2,2,128,128]{4,3,2,1,0:T(8,128)(2,1)S(1)} %pad_maximum_fusion.2.kv.kv0), channel_id=1, source_target_pairs={{0,8},{1,9},{2,10},{3,11},{4,12},{5,13},{6,14},{7,15},{16,24},{17,... | collective-permute-start | bytes 786440 | tf_op jit(solution)/shard_map/ppermute | solution.py:517
  29.2 2.3 %multiply_cosine_fusion = (f32[5,256,64]{2,1,0:T(8,128)S(1)}, f32[5,256,64]{2,1,0:T(8,128)S(1)}) fusion(f32[64]{0:T(128)S(1)} %negate_power_fusion, f32[5,256]{1,0:T(8,128)S(1)} %subtract_convert_fusion), kind=kLoop, calls=%fused_computation.2 | loop fusion | flops 81920 | bytes 660736 | tf_op jit(solution)/shard_map/cos | solution.py:509
  31.5 1.1 pad_maximum_fusion.cs
  32.6 0.8 copy-done.6
  33.4 9.9 %prepare.1 = (bf16[16,256,128]{2,1,0:T(8,128)(2,1)}, bf16[16,256,128]{2,1,0:T(8,128)(2,1)}, f32[16,1,256]{2,1,0:T(1,128)}, f32[16,1,256]{2,1,0:T(1,128)}, f32[16...) custom-call(s32[1,8]{1,0:T(1,128)} %lens.5, s32[16,8]{1,0:T(8,128)} %copy.57.ids, s32[16,8]{1,0:T(8,128)} %copy.58.grades, ...), custom_call_target="tpu_custom_call" | custom-call | tf_op jit(solution)/shard_map/prepare/pallas_call | solution.py:424
  44.3 7.5 %far.1 = (f32[16,128,256]{2,1,0:T(8,128)}, f32[16,1,256]{2,1,0:T(1,128)}, f32[16,1,256]{2,1,0:T(1,128)}, f32[8,128]{1,0:T(8,128)}, s16[1040,128]{1,0:T(8,128)(2,...) custom-call(s32[1,8]{1,0:T(1,128)} %lens.5, f32[1,128]{1,0:T(1,128)} %bitcast.73, ...), custom_call_target="tpu_custom_call" | custom-call | tf_op jit(solution)/shard_map/far/pallas_call | solution.py:450
  51.8 1.3 collective-permute-start.10
  53.1 1.5 %collective-permute-start.11 = (s16[1040,128]{1,0:T(8,128)(2,1)}, s16[1040,128]{1,0:T(8,128)(2,1)S(1)}, u32[]{:S(2)}, u32[]{:S(2)}) collective-permute-start(s16[1040,128]{1,0:T(8,128)(2,1)} %get-tuple-element.47), channel_id=1, source_target_pairs={{6,0},{7,1},{8,2},{9,3},{10,4},{11,5},{12,6},{13,7},{14,8},{15,9},... | collective-permute-start | bytes 798728 | tf_op jit(solution)/shard_map/ppermute | solution.py:517
  54.6 14.3 %near.1 = (bf16[2,16,128,128]{3,2,1,0:T(8,128)(2,1)}, f32[8,128]{1,0:T(8,128)}, s16[1040,128]{1,0:T(8,128)(2,1)}, s16[1040,128]{1,0:T(8,128)(2,1)}, f32[2,256,128]{2,1,0:T(8,128)}, /*index=5*/f32[2,256,128]{2,1,0:T(8,128)}) custom-call(s32[1,8]{1,0:T(1,128)} %lens.5, f32[1,128]{1,0:T(1,128)} %bitcast.77, f32[5,256,128]{2,1,0:T(8,128)} %pad_maximum_fusion.cs, ...), custom_call_target="tpu_custom_call" | custom-call | tf_op jit(solution)/shard_map/near/pallas_call | solution.py:471
  68.9 1.4 collective-permute-start.8
  70.4 1.3 collective-permute-start.9
  72.4 12.5 %collective-permute-done.10.p4 = s16[1040,128]{1,0:T(8,128)(2,1)S(1)} collective-permute-done((s16[1040,128]{1,0:T(8,128)(2,1)}, s16[1040,128]{1,0:T(8,128)(2,1)S(1)}, u32[]{:S(2)}, u32[]{:S(2)}) %collective-permute-start.10) | collective-permute-done | bytes 266272 | tf_op jit(solution)/shard_map/ppermute | solution.py:517
  84.8 5.0 %collective-permute-done.8.p1 = s16[1040,128]{1,0:T(8,128)(2,1)S(1)} collective-permute-done((s16[1040,128]{1,0:T(8,128)(2,1)}, s16[1040,128]{1,0:T(8,128)(2,1)S(1)}, u32[]{:S(2)}, u32[]{:S(2)}) %collective-permute-start.8) | collective-permute-done | bytes 266272 | tf_op jit(solution)/shard_map/ppermute | solution.py:517
  89.9 3.3 %collective-permute-done.9.p2 = s16[1040,128]{1,0:T(8,128)(2,1)S(1)} collective-permute-done((s16[1040,128]{1,0:T(8,128)(2,1)}, s16[1040,128]{1,0:T(8,128)(2,1)S(1)}, u32[]{:S(2)}, u32[]{:S(2)}) %collective-permute-start.9) | collective-permute-done | bytes 266272 | tf_op jit(solution)/shard_map/ppermute | solution.py:517
  93.9 3.1 %finish.1 = (bf16[2,2,128,128]{3,2,1,0:T(8,128)(2,1)}, bf16[2,2,128,128]{3,2,1,0:T(8,128)(2,1)}) custom-call(f32[1,128]{1,0:T(1,128)} %bitcast.74, f32[5,256,128]{2,1,0:T(8,128)} %pad_maximum_fusion.cs, bf16[2,2,2,128,128]{4,3,2,1,0:T(8,128)(2,1)} %copy-done, f32[2,256,128]{2,1,0:T(8,128)} %get-tuple-element.41.dk, f32[2,256,128]{2,1,0:T(8,128)} %get-tuple-element.42.dv, ...), custom_call_target="tpu_custom_call" | custom-call | tf_op jit(solution)/shard_map/finish/pallas_call | solution.py:567
  96.9 6.2 %collective-permute-start.12 = (bf16[2,2,128,128]{3,2,1,0:T(8,128)(2,1)}, bf16[2,2,128,128]{3,2,1,0:T(8,128)(2,1)S(1)}, u32[]{:S(2)}, u32[]{:S(2)}) collective-permute-start(bf16[2,2,128,128]{3,2,1,0:T(8,128)(2,1)} %get-tuple-element.51), channel_id=1, source_target_pairs={{0,1},{1,0},{2,3},{3,2},{4,5},{5,4},{6,7},{7,6},{8,9},{9,8},{10,11... | collective-permute-start | bytes 393224 | tf_op jit(solution)/shard_map/ppermute | solution.py:513
  103.3 0.8 broadcast_in_dim.47
  104.1 27.1 %all-to-all-start = ((f32[256,1,256]{2,1,0:T(1,128)}), f32[256,1,256]{2,1,0:T(1,128)S(1)}, u32[]{:S(2)}, u32[]{:S(2)}) async-start(f32[256,1,256]{2,1,0:T(1,128)} %broadcast_in_dim.47), calls=%async_computation | async-start | bytes 524288 | tf_op jit(solution)/shard_map/all_to_all | solution.py:562
  131.2 0.9 broadcast_select_fusion.1
  132.2 0.8 copy.62
  133.0 0.8 copy.61
  133.9 1.6 %copy.60 = bf16[128,32,128]{2,1,0:T(8,128)(2,1)} copy(bf16[128,32,128]{2,0,1:T(8,128)(2,1)S(1)} %maximum_bitcast_fusion) | data formatting | bytes 2097152
  135.6 11.5 %all-to-all-done = f32[256,1,256]{2,1,0:T(1,128)S(1)} async-done(((f32[256,1,256]{2,1,0:T(1,128)}), f32[256,1,256]{2,1,0:T(1,128)S(1)}, u32[]{:S(2)}, u32[]{:S(2)}) %all-to-all-start) | async-done | bytes 262176 | tf_op jit(solution)/shard_map/all_to_all | solution.py:562
  (68 shorter events, 5.7 us)
Async XLA Ops:
  0.6 4.5 %copy-start.2 = (bf16[128,32,128]{2,1,0:T(8,128)(2,1)S(1)}, bf16[128,32,128]{2,1,0:T(8,128)(2,1)}, u32[]{:S(2)}) copy-start(bf16[128,32,128]{2,1,0:T(8,128)(2,1)} %param.12) | copy-start | bytes 3145732
  1.8 10.3 %collective-permute-start.2 = (bf16[2,2,128,128]{3,2,1,0:T(8,128)(2,1)S(1)}, bf16[2,2,128,128]{3,2,1,0:T(8,128)(2,1)S(1)}, u32[]{:S(2)}, u32[]{:S(2)}) collective-permute-start(bf16[2,2,128,128]{3,2,1,0:T(8,128)(2,1)S(1)} %bitcast.69), channel_id=1, source_target_pairs={{0,1},{1,0},{2,3},{3,2},{4,5},{5,4},{6,7},{7,6},{8,9},{9,8},{10,11... | collective-permute-start | bytes 393224 | tf_op jit(solution)/shard_map/ppermute | solution.py:513
  6.8 1.0 copy-start.13
  6.8 1.4 copy-start.14
  6.9 18.5 %collective-permute-start = (bf16[16,128,128]{2,1,0:T(8,128)(2,1)S(1)}, bf16[16,128,128]{2,1,0:T(8,128)(2,1)S(1)}, u32[]{:S(2)}, u32[]{:S(2)}) collective-permute-start(bf16[16,128,128]{2,1,0:T(8,128)(2,1)S(1)} %bitcast.67), channel_id=1, source_target_pairs={{0,1},{1,0},{2,3},{3,2},{4,5},{5,4},{6,7},{7,6},{8,9},{9,8},{10,11... | collective-permute-start | bytes 1572872 | tf_op jit(solution)/shard_map/ppermute | solution.py:513
  7.2 25.4 %collective-permute-start.1 = (bf16[16,128,128]{2,1,0:T(8,128)(2,1)S(1)}, bf16[16,128,128]{2,1,0:T(8,128)(2,1)S(1)}, u32[]{:S(2)}, u32[]{:S(2)}) collective-permute-start(bf16[16,128,128]{2,1,0:T(8,128)(2,1)S(1)} %bitcast.66), channel_id=1, source_target_pairs={{0,1},{1,0},{2,3},{3,2},{4,5},{5,4},{6,7},{7,6},{8,9},{9,8},{10,11... | collective-permute-start | bytes 1572872 | tf_op jit(solution)/shard_map/ppermute | solution.py:513
  12.2 20.4 %copy-start = (bf16[2,2,2,128,128]{4,3,2,1,0:T(8,128)(2,1)}, bf16[2,2,2,128,128]{4,3,2,1,0:T(8,128)(2,1)S(1)}, u32[]{:S(2)}) copy-start(bf16[2,2,2,128,128]{4,3,2,1,0:T(8,128)(2,1)S(1)} %pad_maximum_fusion.2.kv.kv0) | copy-start | bytes 786436
  12.2 31.1 %collective-permute-start.6 = (bf16[2,2,2,128,128]{4,3,2,1,0:T(8,128)(2,1)S(1)}, bf16[2,2,2,128,128]{4,3,2,1,0:T(8,128)(2,1)S(1)}, u32[]{:S(2)}, u32[]{:S(2)}) collective-permute-start(bf16[2,2,2,128,128]{4,3,2,1,0:T(8,128)(2,1)S(1)} %pad_maximum_fusion.2.kv.kv0), channel_id=1, source_target_pairs={{0,2},{1,3},{2,4},{3,5},{4,6},{5,7},{6,8},{7,9},{8,10},{9,11},{10,... | collective-permute-start | bytes 786440 | tf_op jit(solution)/shard_map/ppermute | solution.py:517
  19.3 24.0 %collective-permute-start.5 = (bf16[2,2,2,128,128]{4,3,2,1,0:T(8,128)(2,1)S(1)}, bf16[2,2,2,128,128]{4,3,2,1,0:T(8,128)(2,1)S(1)}, u32[]{:S(2)}, u32[]{:S(2)}) collective-permute-start(bf16[2,2,2,128,128]{4,3,2,1,0:T(8,128)(2,1)S(1)} %pad_maximum_fusion.2.kv.kv0), channel_id=1, source_target_pairs={{0,4},{1,5},{2,6},{3,7},{4,8},{5,9},{6,10},{7,11},{8,12},{9,13},{1... | collective-permute-start | bytes 786440 | tf_op jit(solution)/shard_map/ppermute | solution.py:517
  22.5 20.8 %collective-permute-start.4 = (bf16[2,2,2,128,128]{4,3,2,1,0:T(8,128)(2,1)S(1)}, bf16[2,2,2,128,128]{4,3,2,1,0:T(8,128)(2,1)S(1)}, u32[]{:S(2)}, u32[]{:S(2)}) collective-permute-start(bf16[2,2,2,128,128]{4,3,2,1,0:T(8,128)(2,1)S(1)} %pad_maximum_fusion.2.kv.kv0), channel_id=1, source_target_pairs={{0,6},{1,7},{2,8},{3,9},{4,10},{5,11},{6,12},{7,13},{8,14},{9,15},... | collective-permute-start | bytes 786440 | tf_op jit(solution)/shard_map/ppermute | solution.py:517
  25.4 7.2 %copy-start.1 = (bf16[16,128,128]{2,1,0:T(8,128)(2,1)}, bf16[16,128,128]{2,1,0:T(8,128)(2,1)S(1)}, u32[]{:S(2)}) copy-start(bf16[16,128,128]{2,1,0:T(8,128)(2,1)S(1)} %collective-permute-done.q_other) | copy-start | bytes 1572868
  25.4 17.9 %collective-permute-start.3 = (bf16[2,2,2,128,128]{4,3,2,1,0:T(8,128)(2,1)S(1)}, bf16[2,2,2,128,128]{4,3,2,1,0:T(8,128)(2,1)S(1)}, u32[]{:S(2)}, u32[]{:S(2)}) collective-permute-start(bf16[2,2,2,128,128]{4,3,2,1,0:T(8,128)(2,1)S(1)} %pad_maximum_fusion.2.kv.kv0), channel_id=1, source_target_pairs={{0,8},{1,9},{2,10},{3,11},{4,12},{5,13},{6,14},{7,15},{16,24},{17,... | collective-permute-start | bytes 786440 | tf_op jit(solution)/shard_map/ppermute | solution.py:517
  32.6 0.8 copy-start.6
  43.2 0.7 copy-start.3
  43.3 0.8 copy-start.4
  43.3 0.9 copy-start.11
  43.3 1.0 copy-start.12
  51.8 33.0 %collective-permute-start.10 = (s16[1040,128]{1,0:T(8,128)(2,1)}, s16[1040,128]{1,0:T(8,128)(2,1)S(1)}, u32[]{:S(2)}, u32[]{:S(2)}) collective-permute-start(s16[1040,128]{1,0:T(8,128)(2,1)} %get-tuple-element.46), channel_id=1, source_target_pairs={{8,0},{9,1},{10,2},{11,3},{12,4},{13,5},{14,6},{15,7},{24,16},{25,... | collective-permute-start | bytes 798728 | tf_op jit(solution)/shard_map/ppermute | solution.py:517
  53.1 31.7 %collective-permute-start.11 = (s16[1040,128]{1,0:T(8,128)(2,1)}, s16[1040,128]{1,0:T(8,128)(2,1)S(1)}, u32[]{:S(2)}, u32[]{:S(2)}) collective-permute-start(s16[1040,128]{1,0:T(8,128)(2,1)} %get-tuple-element.47), channel_id=1, source_target_pairs={{6,0},{7,1},{8,2},{9,3},{10,4},{11,5},{12,6},{13,7},{14,8},{15,9},... | collective-permute-start | bytes 798728 | tf_op jit(solution)/shard_map/ppermute | solution.py:517
  68.9 34.2 %copy-start.5 = (bf16[2,16,128,128]{3,2,1,0:T(8,128)(2,1)S(1)}, bf16[2,16,128,128]{3,2,1,0:T(8,128)(2,1)}, u32[]{:S(2)}) copy-start(bf16[2,16,128,128]{3,2,1,0:T(8,128)(2,1)} %get-tuple-element.40) | copy-start | bytes 3145732
  68.9 20.9 %collective-permute-start.8 = (s16[1040,128]{1,0:T(8,128)(2,1)}, s16[1040,128]{1,0:T(8,128)(2,1)S(1)}, u32[]{:S(2)}, u32[]{:S(2)}) collective-permute-start(s16[1040,128]{1,0:T(8,128)(2,1)} %get-tuple-element.43), channel_id=1, source_target_pairs={{2,0},{3,1},{4,2},{5,3},{6,4},{7,5},{8,6},{9,7},{10,8},{11,9},{12,... | collective-permute-start | bytes 798728 | tf_op jit(solution)/shard_map/ppermute | solution.py:517
  70.4 22.8 %collective-permute-start.9 = (s16[1040,128]{1,0:T(8,128)(2,1)}, s16[1040,128]{1,0:T(8,128)(2,1)S(1)}, u32[]{:S(2)}, u32[]{:S(2)}) collective-permute-start(s16[1040,128]{1,0:T(8,128)(2,1)} %get-tuple-element.44), channel_id=1, source_target_pairs={{4,0},{5,1},{6,2},{7,3},{8,4},{9,5},{10,6},{11,7},{12,8},{13,9},{1... | collective-permute-start | bytes 798728 | tf_op jit(solution)/shard_map/ppermute | solution.py:517
  84.8 8.3 %copy-start.7 = (s16[1040,128]{1,0:T(8,128)(2,1)}, s16[1040,128]{1,0:T(8,128)(2,1)S(1)}, u32[]{:S(2)}) copy-start(s16[1040,128]{1,0:T(8,128)(2,1)S(1)} %collective-permute-done.10.p4) | copy-start | bytes 798724
  84.8 8.3 %copy-start.8 = (s16[1040,128]{1,0:T(8,128)(2,1)}, s16[1040,128]{1,0:T(8,128)(2,1)S(1)}, u32[]{:S(2)}) copy-start(s16[1040,128]{1,0:T(8,128)(2,1)S(1)} %collective-permute-done.11.p3) | copy-start | bytes 798724
  89.9 3.3 %copy-start.9 = (s16[1040,128]{1,0:T(8,128)(2,1)}, s16[1040,128]{1,0:T(8,128)(2,1)S(1)}, u32[]{:S(2)}) copy-start(s16[1040,128]{1,0:T(8,128)(2,1)S(1)} %collective-permute-done.8.p1) | copy-start | bytes 798724
  93.2 0.7 copy-start.10
  96.9 34.3 %collective-permute-start.12 = (bf16[2,2,128,128]{3,2,1,0:T(8,128)(2,1)}, bf16[2,2,128,128]{3,2,1,0:T(8,128)(2,1)S(1)}, u32[]{:S(2)}, u32[]{:S(2)}) collective-permute-start(bf16[2,2,128,128]{3,2,1,0:T(8,128)(2,1)} %get-tuple-element.51), channel_id=1, source_target_pairs={{0,1},{1,0},{2,3},{3,2},{4,5},{5,4},{6,7},{7,6},{8,9},{9,8},{10,11... | collective-permute-start | bytes 393224 | tf_op jit(solution)/shard_map/ppermute | solution.py:513
  103.2 30.6 %collective-permute-start.7 = (bf16[16,128,128]{2,1,0:T(8,128)(2,1)S(1)}, bf16[16,128,128]{2,1,0:T(8,128)(2,1)S(1)}, u32[]{:S(2)}, u32[]{:S(2)}) collective-permute-start(bf16[16,128,128]{2,1,0:T(8,128)(2,1)S(1)} %slice_bitcast_fusion), channel_id=1, source_target_pairs={{0,1},{1,0},{2,3},{3,2},{4,5},{5,4},{6,7},{7,6},{8,9},{9,8},{10,11... | collective-permute-start | bytes 1572872 | tf_op jit(solution)/shard_map/ppermute | solution.py:513
  104.1 43.0 %all-to-all-start = ((f32[256,1,256]{2,1,0:T(1,128)}), f32[256,1,256]{2,1,0:T(1,128)S(1)}, u32[]{:S(2)}, u32[]{:S(2)}) async-start(f32[256,1,256]{2,1,0:T(1,128)} %broadcast_in_dim.47), calls=%async_computation | async-start | bytes 524288 | tf_op jit(solution)/shard_map/all_to_all | solution.py:562

commit v3 on v2

--- a/solution.py
+++ b/solution.py
@@ -35,6 +35,14 @@
     return lax.rsqrt(jnp.mean(x * x, axis=-1, keepdims=True) + EPS)
 
 
+def inv_rms_wide(x):
+    ones = jnp.full((HD, HD), 1.0 / HD, bf16)
+    square = x * x
+    high = square.astype(bf16)
+    low = (square - high.astype(f32)).astype(bf16)
+    return lax.rsqrt(dot(high, ones, ((1,), (0,))) + dot(low, ones, ((1,), (0,))) + EPS)
+
+
 def turn(x):
     return pltpu.roll(x, HD // 2, x.ndim - 1)
 
@@ -45,8 +53,8 @@
     return jnp.where(low, cs, other), jnp.where(low, -other, cs)
 
 
-def norm_rope(x, gain, cosine, sine):
-    xn = x * inv_rms(x) * gain
+def norm_rope(x, r, gain, cosine, sine):
+    xn = x * r * gain
     return xn * cosine + turn(xn) * sine
 
 
@@ -85,7 +93,7 @@
         at = n * BLK + part * TOK
         cosine, sine = tables(cs[k, rows, :])
         x = kv[part, 0, 0].astype(f32)
-        kr[at : at + TOK, :] = norm_rope(x, gain_row, cosine, sine).astype(bf16)
+        kr[at : at + TOK, :] = norm_rope(x, inv_rms_wide(x), gain_row, cosine, sine).astype(bf16)
         vv[at : at + TOK, :] = kv[part, 1, 0]
 
 
@@ -95,7 +103,7 @@
 
 
 def prep_kernel(
-    lens, ids, grades, q_own, q_other, g_own, g_other, q_gain, k_gain, cs, kv,
+    lens, meta, q_own, q_other, g_own, g_other, q_gain, k_gain, cs, kv,
     q_out, g_out, m_out, l_out, d_out, kr_out, kr, vv, bias, weights,
 ):
     head, half = pl.program_id(0), pl.program_id(1)
@@ -103,20 +111,20 @@
 
     @pl.when((half == 0) & (head == 0))
     def _():
-        adv = []
-        pid, grd = ids[...].astype(f32), grades[...].astype(f32)
-        at_row = lax.broadcasted_iota(i32, pid.shape, 0) == row
-        at_col = lax.broadcasted_iota(i32, pid.shape, 1)
-        for j in range(lens.shape[1]):
-            at = at_row & (at_col == j)
-            name = jnp.sum(jnp.where(at, pid, 0.0), keepdims=True)
-            own = jnp.sum(jnp.where(at, grd, 0.0), keepdims=True)
-            same = jnp.where(pid == name, 1.0, 0.0)
-            count = jnp.sum(same, keepdims=True)
-            centre = jnp.sum(same * grd, keepdims=True) / count
-            spread = grd - centre
-            variance = jnp.sum(same * spread * spread, keepdims=True) / count
-            adv.append((own - centre) / jnp.maximum(jnp.sqrt(variance), 1.0))
+        count = meta.shape[1]
+        ids = jnp.broadcast_to(meta[0:1, :], (count, count))
+        same = jnp.where(ids == jnp.transpose(ids), 1.0, 0.0)
+        graded = meta[1:2, :]
+        column = jnp.transpose(jnp.broadcast_to(graded, (count, count)))
+        counted = jnp.sum(same, axis=0, keepdims=True)
+        centre = jnp.sum(same * column, axis=0, keepdims=True) / counted
+        spread = column - centre
+        variance = jnp.sum(same * spread * spread, axis=0, keepdims=True) / counted
+        every = (graded - centre) / jnp.maximum(jnp.sqrt(variance), 1.0)
+        lane = lax.broadcasted_iota(i32, every.shape, 1) - row * lens.shape[1]
+        adv = [
+            jnp.sum(jnp.where(lane == j, every, 0.0), keepdims=True) for j in range(lens.shape[1])
+        ]
         for part in range(2):
             idx = token_base(place, 0, part) + lax.broadcasted_iota(i32, (TOK, HD), 0)
             weight = jnp.zeros((TOK, HD), f32)
@@ -142,7 +150,7 @@
             x = jnp.where(first, q_own[n], q_other[n]).astype(f32)
             g = jnp.where(first, g_own[n], g_other[n]).astype(f32)
             at = slice(e * TOK, (e + 1) * TOK)
-            q_out[two, at, :] = norm_rope(x, q_gain[...], cosine, sine).astype(bf16)
+            q_out[two, at, :] = norm_rope(x, inv_rms(x), q_gain[...], cosine, sine).astype(bf16)
             g_out[two, at, :] = (weights[half] * g).astype(bf16)
         s = dot(kr[...], q_out[two], ((1,), (1,))) + widen(bias.at[half], slice(None))
         dp = dot(vv[...], g_out[two], ((1,), (1,)))
@@ -165,7 +173,7 @@
         x = kv[part, 0, 0].astype(f32)
         incoming = dk[at : at + TOK, :]
         dn = incoming * cosine - turn(incoming) * sine
-        total = total + jnp.sum(dn * (x * inv_rms(x)), axis=0, keepdims=True)
+        total = total + jnp.sum(dn * (x * inv_rms_wide(x)), axis=0, keepdims=True)
     return total * ROOT
 
 
@@ -408,6 +416,10 @@
     return (head, 0, 0)
 
 
+def core_raw(head, half):
+    return (lax.axis_index("ctx") % 2, head, 0, 0)
+
+
 def block_scratch(done, blocks):
     return [
         pltpu.VMEM((blocks * BLK, HD), bf16),
@@ -419,15 +431,15 @@
     ]
 
 
-def prepare(lengths, ids, grades, q_own, q_other, g_own, g_other, q_gain, k_gain, cs, kv):
+def prepare(lengths, meta, q_own, q_other, g_own, g_other, q_gain, k_gain, cs, kv):
     rows = jax.ShapeDtypeStruct((SLOTS, BLK, HD), bf16)
     return pl.pallas_call(
         prep_kernel,
         grid=(HEADS, 2),
         out_shape=[rows, rows, STAT, STAT, STAT, jax.ShapeDtypeStruct((HEADS, BLK, HD), bf16)],
         in_specs=smem(1)
-        + [spec(ids.shape, whole(2))] * 2
-        + [spec(RAW_BLOCK, own_raw)] * 4
+        + [spec(meta.shape, whole(2))]
+        + [spec((None,) + RAW_BLOCK, core_raw), spec(RAW_BLOCK, own_raw)] * 2
         + [spec((1, HD), whole(2))] * 2
         + [spec((1, BLK, HD), whole(3)), spec(KV_BLOCK, kv_at)],
         out_specs=[spec(Q_BLOCK, by_slot)] * 2
@@ -440,8 +452,11 @@
             pltpu.VMEM((2, TOK, HD), f32),
         ],
         compiler_params=VMEM,
+        cost_estimate=pl.CostEstimate(
+            flops=12_000_000_000, bytes_accessed=6 << 20, transcendentals=SLOTS * BLK * BLK
+        ),
         name="prepare",
-    )(lengths, ids, grades, q_own, q_other, g_own, g_other, q_gain, k_gain, cs, kv)
+    )(lengths, meta, q_own, q_other, g_own, g_other, q_gain, k_gain, cs, kv)
 
 
 def far(lengths, k_gain, cs, q, g, stats, kvs):
@@ -480,7 +495,7 @@
         + [spec(Q_BLOCK, by_slot)] * 2
         + [spec(STAT_BLOCK, by_slot)] * 2
         + [spec(DQ_BLOCK, by_slot), spec(TERMS.shape, whole(2))]
-        + [spec(RAW_BLOCK, own_raw)] * 2
+        + [spec((None,) + RAW_BLOCK, core_raw), spec(RAW_BLOCK, own_raw)]
         + [spec((1, 2 * BLK, HD), by_head), spec((1, BLK, HD), by_head)]
         + [spec(KV_BLOCK, kv_at)] * 3,
         out_specs=[spec((1,) + RAW_BLOCK, lambda head, half: (half, head, 0, 0))]
@@ -489,6 +504,9 @@
         + [spec((1, BLK, HD), by_head)] * 2,
         scratch_shapes=block_scratch(3, 3),
         compiler_params=VMEM,
+        cost_estimate=pl.CostEstimate(
+            flops=16_000_000_000, bytes_accessed=8 << 20, transcendentals=SLOTS * 3 * BLK * BLK
+        ),
         name="near",
     )(lengths, q_gain, cs, q, g, lse, mean, dq, terms, q_own, q_other, kr21, kr0, *kvs)
 
@@ -504,9 +522,10 @@
     tri = jnp.arange(lens.shape[1])
     ends = jnp.sum(jnp.where(tri[None, :] <= tri[:, None], lens[0][None, :], 0), axis=1)
     start = jnp.max(jnp.where(index[..., None] >= ends, ends, 0), axis=-1)
-    freqs = jnp.power(1000000.0, -(jnp.arange(HD // 2, dtype=f32) * (2.0 / HD)))
+    lane = jnp.arange(HD, dtype=i32)
+    freqs = jnp.power(1000000.0, -((lane % (HD // 2)).astype(f32) * (2.0 / HD)))
     angles = (index - start).astype(f32)[..., None] * freqs
-    return jnp.concatenate([jnp.cos(angles), jnp.sin(angles)], axis=-1)
+    return jnp.where(lane < HD // 2, jnp.cos(angles), jnp.sin(angles))
 
 
 def swap_cores(x):
@@ -527,26 +546,26 @@
     kv_mine = lax.dynamic_index_in_dim(kv, core, 0, keepdims=False)
     kv_other = swap_cores(lax.dynamic_index_in_dim(kv, 1 - core, 0, keepdims=False))
     own = jnp.stack([kv_mine, kv_other])
-    blocks = [own] + [shift_chips(own, k) for k in range(1, REACH + 1)]
+    blocks = [own, shift_chips(own, 1), shift_chips(own, 2), None, shift_chips(own, 4)]
+    blocks[3] = shift_chips(blocks[1], 2)
 
     heads = HEADS * GROUP
     q_t = queries.transpose(1, 0, 2).reshape(2, heads, TOK, HD)
     g_t = out_grad.transpose(1, 0, 2).reshape(2, heads, TOK, HD)
-    q_own = lax.dynamic_index_in_dim(q_t, core, 0, keepdims=False)
-    g_own = lax.dynamic_index_in_dim(g_t, core, 0, keepdims=False)
     q_other = swap_cores(lax.dynamic_index_in_dim(q_t, 1 - core, 0, keepdims=False))
     g_other = swap_cores(lax.dynamic_index_in_dim(g_t, 1 - core, 0, keepdims=False))
     cs = rope_tables(place, lengths)
+    meta = jnp.stack([prompt_ids.reshape(-1), grades.reshape(-1)]).astype(f32)
 
     q, g, m, l, d, kr0 = prepare(
-        lengths, prompt_ids, grades, q_own, q_other, g_own, g_other, q_gain2, k_gain2, cs, own
+        lengths, meta, q_t, q_other, g_t, g_other, q_gain2, k_gain2, cs, own
     )
     dq, lse, mean, terms, pack4, pack3, kr21 = far(
         lengths, k_gain2, cs, q, g, (m, l, d), [blocks[k] for k in FAR]
     )
     back4, back3 = shift_chips(pack4, -4), shift_chips(pack3, -3)
     q_half, terms, pack2, pack1, dk, dv = near(
-        lengths, q_gain2, cs, q, g, lse, mean, dq, terms, q_own, q_other, kr21, kr0,
+        lengths, q_gain2, cs, q, g, lse, mean, dq, terms, q_t, q_other, kr21, kr0,
         [blocks[k] for k in NEAR],
     )
     back2, back1 = shift_chips(pack2, -2), shift_chips(pack1, -1)
@@ -557,7 +576,6 @@
     q_grad = jnp.concatenate([first, second]).transpose(1, 0, 2)
 
     pair = terms[:2].reshape(1, 2 * HD)
-    pair, back4, back3 = lax.optimization_barrier((pair, back4, back3))
     count = lax.axis_size("dp") * lax.axis_size("ctx")
     gathered = lax.all_to_all(
         jnp.broadcast_to(pair, (count, 2 * HD)), ("dp", "ctx"), 0, 0, tiled=True

time: 149 us -> 134 us (0.90); the launches traced: 148 us -> 135 us
  waiting for transfers between devices: 32.3 us -> 8.98 us
  starting transfers between devices: 59.9 us -> 77.7 us
  local copies, waits for them, and re-layouts: 14.8 us -> 9.68 us
  Pallas kernels: 34.7 us -> 31.4 us
    all_to_all x1, starting transfers between devices: 27.1 us -> 50.1 us  [on_device(): lax.all_to_all(jnp.broadcast_to(pair, (count, 2 * HD)), ('dp', 'ctx'), 0,...]
    ppermute x8, waiting for transfers between devices: 20.8 us -> 1.97 us  [shift_chips(): lax.ppermute(x, 'ctx', [(i, i + 2 * k) for i in range(16) if 0 <= i + 2 *...]
    all_to_all x1, waiting for transfers between devices: 11.5 us -> 5.95 us  [on_device(): lax.all_to_all(jnp.broadcast_to(pair, (count, 2 * HD)), ('dp', 'ctx'), 0,...]
    unnamed x42 -> x46, local copies, waits for them, and re-layouts: 9.99 us -> 5.36 us
    ppermute x5, starting transfers between devices: 10.3 us -> 6 us  [swap_cores(): return lax.ppermute(x, 'ctx', [(i, i ^ 1) for i in range(16)])]
    select_n x0 -> x1, other arithmetic: none -> 3.32 us  [rope_tables(): return jnp.where(lane < HD // 2, jnp.cos(angles), jnp.sin(angles))]
    cos x1 -> x0, other arithmetic: 2.33 us -> none  [rope_tables(): return jnp.concatenate([jnp.cos(angles), jnp.sin(angles)], axis=-1)]
    dynamic_slice x1 -> x0, local copies, waits for them, and re-layouts: 1.59 us -> none  [on_device(): lax.dynamic_index_in_dim(g_t, 1 - core, 0, keepdims=False)]
  transfers between devices with their start and end apart: 14 -> 14, of which waited for: 4 -> 3; matrix products, arithmetic and copies ran while one was open for 10% -> 8% of each run, Pallas kernels for 16% -> 8%
where the time goes in v3:
time: 134 us; the launch traced here: 135 us
  starting transfers between devices  77.7 us (58%)
  Pallas kernels  31.4 us (23%)
  local copies, waits for them, and re-layouts  9.68 us (7%)
  waiting for transfers between devices  8.98 us (7%)
  other arithmetic  5.69 us (4%)
    all_to_all x1, starting transfers between devices, on_device(): lax.all_to_all(jnp.broadcast_to(pair, (count, 2 * HD)), ('dp', 'ctx'), 0,...  50.1 us
    ppermute x8, starting transfers between devices, shift_chips(): lax.ppermute(x, 'ctx', [(i, i + 2 * k) for i in range(16) if 0 <= i + 2 *...  21.6 us
    pallas_call x1, Pallas kernels, near(): pl.pallas_call(near_kernel, grid=(HEADS, 2), out_shape=[jax.ShapeDtypeStr...  14 us
    pallas_call x1, Pallas kernels, prepare(): pl.pallas_call(prep_kernel, grid=(HEADS, 2), out_shape=[rows, rows, STAT,...  8.34 us
    ppermute x5, starting transfers between devices, swap_cores(): return lax.ppermute(x, 'ctx', [(i, i ^ 1) for i in range(16)])  6 us
    pallas_call x1, Pallas kernels, far(): pl.pallas_call(far_kernel, grid=(HEADS, 2), out_shape=[dq, STAT, STAT, TE...  5.97 us
    all_to_all x1, waiting for transfers between devices, on_device(): lax.all_to_all(jnp.broadcast_to(pair, (count, 2 * HD)), ('dp', 'ctx'), 0,...  5.95 us
    unnamed x46, local copies, waits for them, and re-layouts  5.36 us
  transfers between devices with their start and end apart: 14, of which 3 were waited for; matrix products, arithmetic and copies ran while one was open for 8% of the time, Pallas kernels for 8%

profile of v3, /device:TPU:1, one launch (start us, length us, event | category | flops | bytes accessed | tf_op | source)
XLA Modules:
  0.0 134.7 jit_solution(18006381883476622660)
XLA Ops:
  0.7 1.1 copy_bitcast_fusion.2
  1.9 3.3 %collective-permute-start.2 = (bf16[2,2,128,128]{3,2,1,0:T(8,128)(2,1)S(1)}, bf16[2,2,128,128]{3,2,1,0:T(8,128)(2,1)S(1)}, u32[]{:S(2)}, u32[]{:S(2)}) collective-permute-start(bf16[2,2,128,128]{3,2,1,0:T(8,128)(2,1)S(1)} %bitcast.59), channel_id=1, source_target_pairs={{0,1},{1,0},{2,3},{3,2},{4,5},{5,4},{6,7},{7,6},{8,9},{9,8},{10,11... | collective-permute-start | bytes 393224 | tf_op jit(solution)/shard_map/ppermute | solution.py:532
  5.2 0.4 copy.45
  5.8 0.4 copy.46
  7.6 0.6 add_convert_fusion.meta
  8.3 7.1 %collective-permute-start.4 = (bf16[2,2,2,128,128]{4,3,2,1,0:T(8,128)(2,1)S(1)}, bf16[2,2,2,128,128]{4,3,2,1,0:T(8,128)(2,1)S(1)}, u32[]{:S(2)}, u32[]{:S(2)}) collective-permute-start(bf16[2,2,2,128,128]{4,3,2,1,0:T(8,128)(2,1)S(1)} %pad_maximum_fusion.1.kv.kv0), channel_id=1, source_target_pairs={{0,2},{1,3},{2,4},{3,5},{4,6},{5,7},{6,8},{7,9},{8,10},{9,11},{10,... | collective-permute-start | bytes 786440 | tf_op jit(solution)/shard_map/ppermute | solution.py:536
  15.4 3.3 %fusion.cs = f32[5,256,128]{2,1,0:T(8,128)} fusion(f32[128]{0:T(128)S(1)} %fusion.4, f32[5,256]{1,0:T(8,128)S(1)} %subtract_convert_fusion, pred[128]{0:T(512)(128)(4,1)S(1)} %iota_compare_fusion.1), kind=kLoop, calls=%fused_computation.3 | loop fusion | flops 327680 | bytes 661120 | tf_op jit(solution)/shard_map/jit(_where)/select_n | solution.py:528
  18.7 3.2 %collective-permute-start.6 = (bf16[2,2,2,128,128]{4,3,2,1,0:T(8,128)(2,1)S(1)}, bf16[2,2,2,128,128]{4,3,2,1,0:T(8,128)(2,1)S(1)}, u32[]{:S(2)}, u32[]{:S(2)}) collective-permute-start(bf16[2,2,2,128,128]{4,3,2,1,0:T(8,128)(2,1)S(1)} %pad_maximum_fusion.1.kv.kv0), channel_id=1, source_target_pairs={{0,4},{1,5},{2,6},{3,7},{4,8},{5,9},{6,10},{7,11},{8,12},{9,13},{1... | collective-permute-start | bytes 786440 | tf_op jit(solution)/shard_map/ppermute | solution.py:536
  21.9 4.5 %collective-permute-start.3 = (bf16[2,2,2,128,128]{4,3,2,1,0:T(8,128)(2,1)S(1)}, bf16[2,2,2,128,128]{4,3,2,1,0:T(8,128)(2,1)S(1)}, u32[]{:S(2)}, u32[]{:S(2)}) collective-permute-start(bf16[2,2,2,128,128]{4,3,2,1,0:T(8,128)(2,1)S(1)} %pad_maximum_fusion.1.kv.kv0), channel_id=1, source_target_pairs={{0,8},{1,9},{2,10},{3,11},{4,12},{5,13},{6,14},{7,15},{16,24},{17,... | collective-permute-start | bytes 786440 | tf_op jit(solution)/shard_map/ppermute | solution.py:536
  26.5 1.5 %collective-permute-start.5 = (bf16[2,2,2,128,128]{4,3,2,1,0:T(8,128)(2,1)S(1)}, bf16[2,2,2,128,128]{4,3,2,1,0:T(8,128)(2,1)S(1)}, u32[]{:S(2)}, u32[]{:S(2)}) collective-permute-start(bf16[2,2,2,128,128]{4,3,2,1,0:T(8,128)(2,1)S(1)} %collective-permute-done.4.kv1), channel_id=1, source_target_pairs={{0,4},{1,5},{2,6},{3,7},{4,8},{5,9},{6,10},{7,11},{8,12},{9,13},{1... | collective-permute-start | bytes 786440 | tf_op jit(solution)/shard_map/ppermute | solution.py:536
  28.0 8.3 %prepare.1 = (bf16[16,256,128]{2,1,0:T(8,128)(2,1)}, bf16[16,256,128]{2,1,0:T(8,128)(2,1)}, f32[16,1,256]{2,1,0:T(1,128)}, f32[16,1,256]{2,1,0:T(1,128)}, f32[16...) custom-call(s32[1,8]{1,0:T(1,128)} %lens.5, f32[2,128]{1,0:T(2,128)} %add_convert_fusion.meta, ...), custom_call_target="tpu_custom_call" | custom-call | flops 12000000000 | bytes 6291456 | tf_op jit(solution)/shard_map/prepare/pallas_call | solution.py:436
  36.4 2.0 %collective-permute-done.5.kv3 = bf16[2,2,2,128,128]{4,3,2,1,0:T(8,128)(2,1)S(1)} collective-permute-done((bf16[2,2,2,128,128]{4,3,2,1,0:T(8,128)(2,1)S(1)}, bf16[2,2,2,128,128]{4,3,2,1,0:T(8,128)(2,1)S(1)}, u32[]{:S(2)}, u32[]{:S(2)}) %collective-permute-start.5) | collective-permute-done | bytes 262176 | tf_op jit(solution)/shard_map/ppermute | solution.py:536
  38.4 0.7 copy-done.13
  39.1 6.0 %far.1 = (f32[16,128,256]{2,1,0:T(8,128)}, f32[16,1,256]{2,1,0:T(1,128)}, f32[16,1,256]{2,1,0:T(1,128)}, f32[8,128]{1,0:T(8,128)}, s16[1040,128]{1,0:T(8,128)(2,...) custom-call(s32[1,8]{1,0:T(1,128)} %lens.5, f32[1,128]{1,0:T(1,128)} %bitcast.62, f32[5,256,128]{2,1,0:T(8,128)} %fusion.cs, ...), custom_call_target="tpu_custom_call" | custom-call | tf_op jit(solution)/shard_map/far/pallas_call | solution.py:465
  45.1 14.0 %near.1 = (bf16[2,16,128,128]{3,2,1,0:T(8,128)(2,1)}, f32[8,128]{1,0:T(8,128)}, s16[1040,128]{1,0:T(8,128)(2,1)}, s16[1040,128]{1,0:T(8,128)(2,1)}, f32[2,256,128]{2,1,0:T(8,128)}, /*index=5*/f32[2,256,128]{2,1,0:T(8,128)}) custom-call(s32[1,8]{1,0:T(1,128)} %lens.5, f32[1,128]{1,0:T(1,128)} %bitcast.66, f32[5,256,128]{2,1,0:T(8,128)} %fusion.cs, ...), custom_call_target="tpu_custom_call" | custom-call | flops 16000000000 | bytes 8388608 | tf_op jit(solution)/shard_map/near/pallas_call | solution.py:486
  59.1 1.4 %collective-permute-start.8 = (s16[1040,128]{1,0:T(8,128)(2,1)}, s16[1040,128]{1,0:T(8,128)(2,1)S(1)}, u32[]{:S(2)}, u32[]{:S(2)}) collective-permute-start(s16[1040,128]{1,0:T(8,128)(2,1)} %get-tuple-element.40), channel_id=1, source_target_pairs={{2,0},{3,1},{4,2},{5,3},{6,4},{7,5},{8,6},{9,7},{10,8},{11,9},{12,... | collective-permute-start | bytes 798728 | tf_op jit(solution)/shard_map/ppermute | solution.py:536
  60.6 1.3 collective-permute-start.9
  61.9 1.3 collective-permute-start.10
  63.2 1.3 collective-permute-start.11
  64.5 0.7 slice_bitcast_fusion.3
  65.2 0.8 broadcast_in_dim.55
  66.0 50.1 %all-to-all-start = ((f32[256,1,256]{2,1,0:T(1,128)}), f32[256,1,256]{2,1,0:T(1,128)S(1)}, u32[]{:S(2)}, u32[]{:S(2)}) async-start(f32[256,1,256]{2,1,0:T(1,128)} %broadcast_in_dim.55), calls=%async_computation | async-start | bytes 524288 | tf_op jit(solution)/shard_map/all_to_all | solution.py:580
  116.2 0.6 copy-done.6
  117.1 3.1 %finish.1 = (bf16[2,2,128,128]{3,2,1,0:T(8,128)(2,1)}, bf16[2,2,128,128]{3,2,1,0:T(8,128)(2,1)}) custom-call(f32[1,128]{1,0:T(1,128)} %bitcast.63, f32[5,256,128]{2,1,0:T(8,128)} %fusion.cs, bf16[2,2,2,128,128]{4,3,2,1,0:T(8,128)(2,1)} %copy-done.5, f32[2,256,128]{2,1,0:T(8,128)} %get-tuple-element.38.dk, f32[2,256,128]{2,1,0:T(8,128)} %get-tuple-element.39.dv, ...), custom_call_target="tpu_custom_call" | custom-call | tf_op jit(solution)/shard_map/finish/pallas_call | solution.py:585
  120.2 2.1 %collective-permute-start.12 = (bf16[2,2,128,128]{3,2,1,0:T(8,128)(2,1)}, bf16[2,2,128,128]{3,2,1,0:T(8,128)(2,1)S(1)}, u32[]{:S(2)}, u32[]{:S(2)}) collective-permute-start(bf16[2,2,128,128]{3,2,1,0:T(8,128)(2,1)} %get-tuple-element.45), channel_id=1, source_target_pairs={{0,1},{1,0},{2,3},{3,2},{4,5},{5,4},{6,7},{7,6},{8,9},{9,8},{10,11... | collective-permute-start | bytes 393224 | tf_op jit(solution)/shard_map/ppermute | solution.py:532
  122.5 1.0 collective-permute-done.12
  123.5 0.9 broadcast_select_fusion.1
  124.5 0.8 copy.54
  125.3 0.8 copy.53
  126.1 6.0 %all-to-all-done = f32[256,1,256]{2,1,0:T(1,128)S(1)} async-done(((f32[256,1,256]{2,1,0:T(1,128)}), f32[256,1,256]{2,1,0:T(1,128)S(1)}, u32[]{:S(2)}, u32[]{:S(2)}) %all-to-all-start) | async-done | bytes 262176 | tf_op jit(solution)/shard_map/all_to_all | solution.py:580
  132.3 0.5 fusion.5
  133.0 1.6 %copy.52 = bf16[128,32,128]{2,1,0:T(8,128)(2,1)} copy(bf16[128,32,128]{2,0,1:T(8,128)(2,1)S(1)} %maximum_bitcast_fusion) | data formatting | bytes 2097152
  (78 shorter events, 2.6 us)
Async XLA Ops:
  0.6 4.6 %copy-start.3 = (bf16[128,32,128]{2,1,0:T(8,128)(2,1)S(1)}, bf16[128,32,128]{2,1,0:T(8,128)(2,1)}, u32[]{:S(2)}) copy-start(bf16[128,32,128]{2,1,0:T(8,128)(2,1)} %param.9) | copy-start | bytes 3145732
  1.8 4.0 %copy-start.4 = (bf16[128,32,128]{2,1,0:T(8,128)(2,1)S(1)}, bf16[128,32,128]{2,1,0:T(8,128)(2,1)}, u32[]{:S(2)}) copy-start(bf16[128,32,128]{2,1,0:T(8,128)(2,1)} %param.12) | copy-start | bytes 3145732
  1.9 6.4 %collective-permute-start.2 = (bf16[2,2,128,128]{3,2,1,0:T(8,128)(2,1)S(1)}, bf16[2,2,128,128]{3,2,1,0:T(8,128)(2,1)S(1)}, u32[]{:S(2)}, u32[]{:S(2)}) collective-permute-start(bf16[2,2,128,128]{3,2,1,0:T(8,128)(2,1)S(1)} %bitcast.59), channel_id=1, source_target_pairs={{0,1},{1,0},{2,3},{3,2},{4,5},{5,4},{6,7},{7,6},{8,9},{9,8},{10,11... | collective-permute-start | bytes 393224 | tf_op jit(solution)/shard_map/ppermute | solution.py:532
  5.6 1.0 copy-start
  5.6 1.3 copy-start.16
  5.6 1.7 %copy-start.14 = (s32[16,8]{0,1:T(8,128)S(1)}, s32[16,8]{0,1:T(8,128)}, u32[]{:S(2)}) copy-start(s32[16,8]{0,1:T(8,128)} %param.16) | copy-start | bytes 1540
  5.6 1.8 %copy-start.15 = (s32[16,8]{0,1:T(8,128)S(1)}, s32[16,8]{0,1:T(8,128)}, u32[]{:S(2)}) copy-start(s32[16,8]{0,1:T(8,128)} %param.17) | copy-start | bytes 1540
  5.7 22.3 %collective-permute-start = (bf16[16,128,128]{2,1,0:T(8,128)(2,1)S(1)}, bf16[16,128,128]{2,1,0:T(8,128)(2,1)}, u32[]{:S(2)}, u32[]{:S(2)}) collective-permute-start(bf16[16,128,128]{2,1,0:T(8,128)(2,1)S(1)} %dynamic-slice_bitcast_fusion.1), channel_id=1, source_target_pairs={{0,1},{1,0},{2,3},{3,2},{4,5},{5,4},{6,7},{7,6},{8,9},{9,8},{10,11... | collective-permute-start | bytes 1572872 | tf_op jit(solution)/shard_map/ppermute | solution.py:532
  6.2 21.8 %copy-start.1 = (bf16[32,128,128]{2,1,0:T(8,128)(2,1)}, bf16[32,128,128]{2,1,0:T(8,128)(2,1)S(1)}, u32[]{:S(2)}) copy-start(bf16[32,128,128]{2,1,0:T(8,128)(2,1)S(1)} %copy.46) | copy-start | bytes 3145732
  6.6 21.4 %collective-permute-start.1 = (bf16[16,128,128]{2,1,0:T(8,128)(2,1)S(1)}, bf16[16,128,128]{2,1,0:T(8,128)(2,1)}, u32[]{:S(2)}, u32[]{:S(2)}) collective-permute-start(bf16[16,128,128]{2,1,0:T(8,128)(2,1)S(1)} %dynamic-slice_bitcast_fusion), channel_id=1, source_target_pairs={{0,1},{1,0},{2,3},{3,2},{4,5},{5,4},{6,7},{7,6},{8,9},{9,8},{10,11... | collective-permute-start | bytes 1572872 | tf_op jit(solution)/shard_map/ppermute | solution.py:532
  8.3 19.7 %copy-start.5 = (bf16[2,2,2,128,128]{4,3,2,1,0:T(8,128)(2,1)}, bf16[2,2,2,128,128]{4,3,2,1,0:T(8,128)(2,1)S(1)}, u32[]{:S(2)}) copy-start(bf16[2,2,2,128,128]{4,3,2,1,0:T(8,128)(2,1)S(1)} %pad_maximum_fusion.1.kv.kv0) | copy-start | bytes 786436
  8.3 18.2 %collective-permute-start.4 = (bf16[2,2,2,128,128]{4,3,2,1,0:T(8,128)(2,1)S(1)}, bf16[2,2,2,128,128]{4,3,2,1,0:T(8,128)(2,1)S(1)}, u32[]{:S(2)}, u32[]{:S(2)}) collective-permute-start(bf16[2,2,2,128,128]{4,3,2,1,0:T(8,128)(2,1)S(1)} %pad_maximum_fusion.1.kv.kv0), channel_id=1, source_target_pairs={{0,2},{1,3},{2,4},{3,5},{4,6},{5,7},{6,8},{7,9},{8,10},{9,11},{10,... | collective-permute-start | bytes 786440 | tf_op jit(solution)/shard_map/ppermute | solution.py:536
  18.7 17.6 %collective-permute-start.6 = (bf16[2,2,2,128,128]{4,3,2,1,0:T(8,128)(2,1)S(1)}, bf16[2,2,2,128,128]{4,3,2,1,0:T(8,128)(2,1)S(1)}, u32[]{:S(2)}, u32[]{:S(2)}) collective-permute-start(bf16[2,2,2,128,128]{4,3,2,1,0:T(8,128)(2,1)S(1)} %pad_maximum_fusion.1.kv.kv0), channel_id=1, source_target_pairs={{0,4},{1,5},{2,6},{3,7},{4,8},{5,9},{6,10},{7,11},{8,12},{9,13},{1... | collective-permute-start | bytes 786440 | tf_op jit(solution)/shard_map/ppermute | solution.py:536
  21.9 14.5 %collective-permute-start.3 = (bf16[2,2,2,128,128]{4,3,2,1,0:T(8,128)(2,1)S(1)}, bf16[2,2,2,128,128]{4,3,2,1,0:T(8,128)(2,1)S(1)}, u32[]{:S(2)}, u32[]{:S(2)}) collective-permute-start(bf16[2,2,2,128,128]{4,3,2,1,0:T(8,128)(2,1)S(1)} %pad_maximum_fusion.1.kv.kv0), channel_id=1, source_target_pairs={{0,8},{1,9},{2,10},{3,11},{4,12},{5,13},{6,14},{7,15},{16,24},{17,... | collective-permute-start | bytes 786440 | tf_op jit(solution)/shard_map/ppermute | solution.py:536
  26.5 9.9 %copy-start.10 = (bf16[2,2,2,128,128]{4,3,2,1,0:T(8,128)(2,1)}, bf16[2,2,2,128,128]{4,3,2,1,0:T(8,128)(2,1)S(1)}, u32[]{:S(2)}) copy-start(bf16[2,2,2,128,128]{4,3,2,1,0:T(8,128)(2,1)S(1)} %collective-permute-done.4.kv1) | copy-start | bytes 786436
  26.5 11.9 %collective-permute-start.5 = (bf16[2,2,2,128,128]{4,3,2,1,0:T(8,128)(2,1)S(1)}, bf16[2,2,2,128,128]{4,3,2,1,0:T(8,128)(2,1)S(1)}, u32[]{:S(2)}, u32[]{:S(2)}) collective-permute-start(bf16[2,2,2,128,128]{4,3,2,1,0:T(8,128)(2,1)S(1)} %collective-permute-done.4.kv1), channel_id=1, source_target_pairs={{0,4},{1,5},{2,6},{3,7},{4,8},{5,9},{6,10},{7,11},{8,12},{9,13},{1... | collective-permute-start | bytes 786440 | tf_op jit(solution)/shard_map/ppermute | solution.py:536
  36.4 2.0 %copy-start.11 = (bf16[2,2,2,128,128]{4,3,2,1,0:T(8,128)(2,1)}, bf16[2,2,2,128,128]{4,3,2,1,0:T(8,128)(2,1)S(1)}, u32[]{:S(2)}) copy-start(bf16[2,2,2,128,128]{4,3,2,1,0:T(8,128)(2,1)S(1)} %collective-permute-done.6.kv2) | copy-start | bytes 786436
  36.4 2.0 %copy-start.12 = (bf16[2,2,2,128,128]{4,3,2,1,0:T(8,128)(2,1)}, bf16[2,2,2,128,128]{4,3,2,1,0:T(8,128)(2,1)S(1)}, u32[]{:S(2)}) copy-start(bf16[2,2,2,128,128]{4,3,2,1,0:T(8,128)(2,1)S(1)} %collective-permute-done.3.kv4) | copy-start | bytes 786436
  38.4 0.7 copy-start.13
  45.1 16.8 %copy-start.18 = (s16[1040,128]{1,0:T(8,128)(2,1)S(1)}, s16[1040,128]{1,0:T(8,128)(2,1)}, u32[]{:S(2)}) copy-start(s16[1040,128]{1,0:T(8,128)(2,1)} %get-tuple-element.42) | copy-start | bytes 798724
  45.1 18.1 %copy-start.17 = (s16[1040,128]{1,0:T(8,128)(2,1)S(1)}, s16[1040,128]{1,0:T(8,128)(2,1)}, u32[]{:S(2)}) copy-start(s16[1040,128]{1,0:T(8,128)(2,1)} %get-tuple-element.43) | copy-start | bytes 798724
  59.1 63.2 %copy-start.2 = (bf16[2,16,128,128]{3,2,1,0:T(8,128)(2,1)S(1)}, bf16[2,16,128,128]{3,2,1,0:T(8,128)(2,1)}, u32[]{:S(2)}) copy-start(bf16[2,16,128,128]{3,2,1,0:T(8,128)(2,1)} %get-tuple-element.37) | copy-start | bytes 3145732
  59.1 57.0 %collective-permute-start.8 = (s16[1040,128]{1,0:T(8,128)(2,1)}, s16[1040,128]{1,0:T(8,128)(2,1)S(1)}, u32[]{:S(2)}, u32[]{:S(2)}) collective-permute-start(s16[1040,128]{1,0:T(8,128)(2,1)} %get-tuple-element.40), channel_id=1, source_target_pairs={{2,0},{3,1},{4,2},{5,3},{6,4},{7,5},{8,6},{9,7},{10,8},{11,9},{12,... | collective-permute-start | bytes 798728 | tf_op jit(solution)/shard_map/ppermute | solution.py:536
  60.6 55.6 %collective-permute-start.9 = (s16[1040,128]{1,0:T(8,128)(2,1)}, s16[1040,128]{1,0:T(8,128)(2,1)S(1)}, u32[]{:S(2)}, u32[]{:S(2)}) collective-permute-start(s16[1040,128]{1,0:T(8,128)(2,1)} %get-tuple-element.41), channel_id=1, source_target_pairs={{4,0},{5,1},{6,2},{7,3},{8,4},{9,5},{10,6},{11,7},{12,8},{13,9},{1... | collective-permute-start | bytes 798728 | tf_op jit(solution)/shard_map/ppermute | solution.py:536
  61.9 54.3 %collective-permute-start.10 = (s16[1040,128]{1,0:T(8,128)(2,1)S(1)}, s16[1040,128]{1,0:T(8,128)(2,1)S(1)}, u32[]{:S(2)}, u32[]{:S(2)}) collective-permute-start(s16[1040,128]{1,0:T(8,128)(2,1)S(1)} %copy-done.18), channel_id=1, source_target_pairs={{6,0},{7,1},{8,2},{9,3},{10,4},{11,5},{12,6},{13,7},{14,8},{15,9},... | collective-permute-start | bytes 798728 | tf_op jit(solution)/shard_map/ppermute | solution.py:536
  63.2 53.0 %collective-permute-start.11 = (s16[1040,128]{1,0:T(8,128)(2,1)S(1)}, s16[1040,128]{1,0:T(8,128)(2,1)S(1)}, u32[]{:S(2)}, u32[]{:S(2)}) collective-permute-start(s16[1040,128]{1,0:T(8,128)(2,1)S(1)} %copy-done.17), channel_id=1, source_target_pairs={{8,0},{9,1},{10,2},{11,3},{12,4},{13,5},{14,6},{15,7},{24,16},{25,... | collective-permute-start | bytes 798728 | tf_op jit(solution)/shard_map/ppermute | solution.py:536
  66.0 66.0 %all-to-all-start = ((f32[256,1,256]{2,1,0:T(1,128)}), f32[256,1,256]{2,1,0:T(1,128)S(1)}, u32[]{:S(2)}, u32[]{:S(2)}) async-start(f32[256,1,256]{2,1,0:T(1,128)} %broadcast_in_dim.55), calls=%async_computation | async-start | bytes 524288 | tf_op jit(solution)/shard_map/all_to_all | solution.py:580
  116.2 0.8 copy-start.7
  116.2 0.8 copy-start.8
  116.2 0.9 copy-start.9
  120.2 3.3 %collective-permute-start.12 = (bf16[2,2,128,128]{3,2,1,0:T(8,128)(2,1)}, bf16[2,2,128,128]{3,2,1,0:T(8,128)(2,1)S(1)}, u32[]{:S(2)}, u32[]{:S(2)}) collective-permute-start(bf16[2,2,128,128]{3,2,1,0:T(8,128)(2,1)} %get-tuple-element.45), channel_id=1, source_target_pairs={{0,1},{1,0},{2,3},{3,2},{4,5},{5,4},{6,7},{7,6},{8,9},{9,8},{10,11... | collective-permute-start | bytes 393224 | tf_op jit(solution)/shard_map/ppermute | solution.py:532
  122.4 10.4 %collective-permute-start.7 = (bf16[16,128,128]{2,1,0:T(8,128)(2,1)S(1)}, bf16[16,128,128]{2,1,0:T(8,128)(2,1)S(1)}, u32[]{:S(2)}, u32[]{:S(2)}) collective-permute-start(bf16[16,128,128]{2,1,0:T(8,128)(2,1)S(1)} %slice_bitcast_fusion), channel_id=1, source_target_pairs={{0,1},{1,0},{2,3},{3,2},{4,5},{5,4},{6,7},{7,6},{8,9},{9,8},{10,11... | collective-permute-start | bytes 1572872 | tf_op jit(solution)/shard_map/ppermute | solution.py:532
  (1 other events, 0.7 us)

commit v4 on v3

--- a/solution.py
+++ b/solution.py
@@ -22,7 +22,7 @@
 UNROLL = 4
 QMAX = 32000.0
 GAP_MAX = 64.0 / EXP_SCALE
-VMEM = pltpu.CompilerParams(vmem_limit_bytes=56 * 1024 * 1024)
+VMEM = pltpu.CompilerParams(vmem_limit_bytes=24 * 1024 * 1024)
 
 f32, bf16, i32 = jnp.float32, jnp.bfloat16, jnp.int32
 

time: 134 us -> 133 us (level); the launches traced: 135 us -> 132 us
  Pallas kernels: 31.4 us -> 24.8 us
  waiting for transfers between devices: 8.98 us -> 14.1 us
  other arithmetic: 5.69 us -> 4.2 us
    ppermute x8, waiting for transfers between devices: 1.97 us -> 4.9 us  [shift_chips(): lax.ppermute(x, 'ctx', [(i, i + 2 * k) for i in range(16) if 0 <= i + 2 *...]
    all_to_all x1, waiting for transfers between devices: 5.95 us -> 8.35 us  [on_device(): lax.all_to_all(jnp.broadcast_to(pair, (count, 2 * HD)), ('dp', 'ctx'), 0,...]
    pallas_call x1, Pallas kernels: 3.07 us -> 0.71 us  [on_device(): pl.pallas_call(finish_kernel, out_shape=[jax.ShapeDtypeStruct((2, HEADS,...]
    pallas_call x1, Pallas kernels: 5.97 us -> 3.94 us  [far(): pl.pallas_call(far_kernel, grid=(HEADS, 2), out_shape=[dq, STAT, STAT, TE...]
    unnamed x46 -> x26, local copies, waits for them, and re-layouts: 5.36 us -> 5.09 us
  transfers between devices with their start and end apart: 14 -> 14, of which waited for: 3 -> 3; matrix products, arithmetic and copies ran while one was open for 8% -> 7% of each run, Pallas kernels for 8% -> 6%
where the time goes in v4:
time: 133 us; the launch traced here: 132 us
  starting transfers between devices  77.3 us (58%)
  Pallas kernels  24.8 us (19%)
  waiting for transfers between devices  14.1 us (11%)
  local copies, waits for them, and re-layouts  10.3 us (8%)
  other arithmetic  4.2 us (3%)
    all_to_all x1, starting transfers between devices, on_device(): lax.all_to_all(jnp.broadcast_to(pair, (count, 2 * HD)), ('dp', 'ctx'), 0,...  49.6 us
    ppermute x8, starting transfers between devices, shift_chips(): lax.ppermute(x, 'ctx', [(i, i + 2 * k) for i in range(16) if 0 <= i + 2 *...  21.5 us
    pallas_call x1, Pallas kernels, near(): pl.pallas_call(near_kernel, grid=(HEADS, 2), out_shape=[jax.ShapeDtypeStr...  12.9 us
    all_to_all x1, waiting for transfers between devices, on_device(): lax.all_to_all(jnp.broadcast_to(pair, (count, 2 * HD)), ('dp', 'ctx'), 0,...  8.35 us
    pallas_call x1, Pallas kernels, prepare(): pl.pallas_call(prep_kernel, grid=(HEADS, 2), out_shape=[rows, rows, STAT,...  7.19 us
    ppermute x5, starting transfers between devices, swap_cores(): return lax.ppermute(x, 'ctx', [(i, i ^ 1) for i in range(16)])  6.24 us
    unnamed x26, local copies, waits for them, and re-layouts  5.09 us
    ppermute x8, waiting for transfers between devices, shift_chips(): lax.ppermute(x, 'ctx', [(i, i + 2 * k) for i in range(16) if 0 <= i + 2 *...  4.9 us
  transfers between devices with their start and end apart: 14, of which 3 were waited for; matrix products, arithmetic and copies ran while one was open for 7% of the time, Pallas kernels for 6%

profile of v4, /device:TPU:1, one launch (start us, length us, event | category | flops | bytes accessed | tf_op | source)
XLA Modules:
  0.0 131.7 jit_solution(4126752171922784552)
XLA Ops:
  0.7 1.1 copy_bitcast_fusion.2
  1.9 3.3 %collective-permute-start.2 = (bf16[2,2,128,128]{3,2,1,0:T(8,128)(2,1)S(1)}, bf16[2,2,128,128]{3,2,1,0:T(8,128)(2,1)S(1)}, u32[]{:S(2)}, u32[]{:S(2)}) collective-permute-start(bf16[2,2,128,128]{3,2,1,0:T(8,128)(2,1)S(1)} %bitcast.65), channel_id=1, source_target_pairs={{0,1},{1,0},{2,3},{3,2},{4,5},{5,4},{6,7},{7,6},{8,9},{9,8},{10,11... | collective-permute-start | bytes 393224 | tf_op jit(solution)/shard_map/ppermute | solution.py:532
  5.2 0.4 copy.45
  5.6 0.8 dynamic-slice_bitcast_fusion.1
  6.9 0.8 dynamic-slice_bitcast_fusion
  7.8 0.5 collective-permute-start.1
  9.1 7.1 %collective-permute-start.4 = (bf16[2,2,2,128,128]{4,3,2,1,0:T(8,128)(2,1)S(1)}, bf16[2,2,2,128,128]{4,3,2,1,0:T(8,128)(2,1)S(1)}, u32[]{:S(2)}, u32[]{:S(2)}) collective-permute-start(bf16[2,2,2,128,128]{4,3,2,1,0:T(8,128)(2,1)S(1)} %pad_maximum_fusion.1.kv.kv0), channel_id=1, source_target_pairs={{0,2},{1,3},{2,4},{3,5},{4,6},{5,7},{6,8},{7,9},{8,10},{9,11},{10,... | collective-permute-start | bytes 786440 | tf_op jit(solution)/shard_map/ppermute | solution.py:536
  16.2 2.4 %fusion.cs = f32[5,256,128]{2,1,0:T(8,128)S(1)} fusion(f32[128]{0:T(128)S(1)} %fusion.4, f32[5,256]{1,0:T(8,128)S(1)} %subtract_convert_fusion, pred[128]{0:T(512)(128)(4,1)S(1)} %iota_compare_fusion.1), kind=kLoop, calls=%fused_computation.3 | loop fusion | flops 327680 | bytes 661120 | tf_op jit(solution)/shard_map/jit(_where)/select_n | solution.py:528
  18.6 3.2 %collective-permute-start.6 = (bf16[2,2,2,128,128]{4,3,2,1,0:T(8,128)(2,1)S(1)}, bf16[2,2,2,128,128]{4,3,2,1,0:T(8,128)(2,1)S(1)}, u32[]{:S(2)}, u32[]{:S(2)}) collective-permute-start(bf16[2,2,2,128,128]{4,3,2,1,0:T(8,128)(2,1)S(1)} %pad_maximum_fusion.1.kv.kv0), channel_id=1, source_target_pairs={{0,4},{1,5},{2,6},{3,7},{4,8},{5,9},{6,10},{7,11},{8,12},{9,13},{1... | collective-permute-start | bytes 786440 | tf_op jit(solution)/shard_map/ppermute | solution.py:536
  21.8 4.5 %collective-permute-start.3 = (bf16[2,2,2,128,128]{4,3,2,1,0:T(8,128)(2,1)S(1)}, bf16[2,2,2,128,128]{4,3,2,1,0:T(8,128)(2,1)S(1)}, u32[]{:S(2)}, u32[]{:S(2)}) collective-permute-start(bf16[2,2,2,128,128]{4,3,2,1,0:T(8,128)(2,1)S(1)} %pad_maximum_fusion.1.kv.kv0), channel_id=1, source_target_pairs={{0,8},{1,9},{2,10},{3,11},{4,12},{5,13},{6,14},{7,15},{16,24},{17,... | collective-permute-start | bytes 786440 | tf_op jit(solution)/shard_map/ppermute | solution.py:536
  26.3 1.5 %collective-permute-start.5 = (bf16[2,2,2,128,128]{4,3,2,1,0:T(8,128)(2,1)S(1)}, bf16[2,2,2,128,128]{4,3,2,1,0:T(8,128)(2,1)S(1)}, u32[]{:S(2)}, u32[]{:S(2)}) collective-permute-start(bf16[2,2,2,128,128]{4,3,2,1,0:T(8,128)(2,1)S(1)} %collective-permute-done.4.kv1), channel_id=1, source_target_pairs={{0,4},{1,5},{2,6},{3,7},{4,8},{5,9},{6,10},{7,11},{8,12},{9,13},{1... | collective-permute-start | bytes 786440 | tf_op jit(solution)/shard_map/ppermute | solution.py:536
  27.9 7.2 %prepare.1 = (bf16[16,256,128]{2,1,0:T(8,128)(2,1)S(1)}, bf16[16,256,128]{2,1,0:T(8,128)(2,1)S(1)}, f32[16,1,256]{2,1,0:T(1,128)S(1)}, f32[16,1,256]{2,1,0:T(1,1...) custom-call(s32[1,8]{1,0:T(1,128)S(1)} %copy-done.3, f32[2,128]{1,0:T(2,128)S(1)} %add_convert_fusion.meta, ...), custom_call_target="tpu_custom_call" | custom-call | flops 12000000000 | bytes 6291456 | tf_op jit(solution)/shard_map/prepare/pallas_call | solution.py:436
  35.1 4.9 %collective-permute-done.5.kv3 = bf16[2,2,2,128,128]{4,3,2,1,0:T(8,128)(2,1)S(1)} collective-permute-done((bf16[2,2,2,128,128]{4,3,2,1,0:T(8,128)(2,1)S(1)}, bf16[2,2,2,128,128]{4,3,2,1,0:T(8,128)(2,1)S(1)}, u32[]{:S(2)}, u32[]{:S(2)}) %collective-permute-start.5) | collective-permute-done | bytes 262176 | tf_op jit(solution)/shard_map/ppermute | solution.py:536
  40.0 3.9 %far.1 = (f32[16,128,256]{2,1,0:T(8,128)S(1)}, f32[16,1,256]{2,1,0:T(1,128)S(1)}, f32[16,1,256]{2,1,0:T(1,128)S(1)}, f32[8,128]{1,0:T(8,128)S(1)}, s16[1040,128]...) custom-call(s32[1,8]{1,0:T(1,128)S(1)} %copy-done.3, f32[1,128]{1,0:T(1,128)S(1)} %bitcast.56, ...), custom_call_target="tpu_custom_call" | custom-call | tf_op jit(solution)/shard_map/far/pallas_call | solution.py:465
  43.9 12.9 %near.1 = (bf16[2,16,128,128]{3,2,1,0:T(8,128)(2,1)S(1)}, f32[8,128]{1,0:T(8,128)S(1)}, s16[1040,128]{1,0:T(8,128)(2,1)}, s16[1040,128]{1,0:T(8,128)(2,1)}, f32[...) custom-call(s32[1,8]{1,0:T(1,128)S(1)} %copy-done.3, f32[1,128]{1,0:T(1,128)S(1)} %bitcast.60, ...), custom_call_target="tpu_custom_call" | custom-call | flops 16000000000 | bytes 8388608 | tf_op jit(solution)/shard_map/near/pallas_call | solution.py:486
  56.8 0.7 copy-done
  57.5 1.3 collective-permute-start.8
  58.8 1.3 collective-permute-start.9
  60.1 1.3 collective-permute-start.10
  61.4 1.3 collective-permute-start.11
  62.8 0.8 broadcast_in_dim.55
  63.6 49.6 %all-to-all-start = ((f32[256,1,256]{2,1,0:T(1,128)}), f32[256,1,256]{2,1,0:T(1,128)}, u32[]{:S(2)}, u32[]{:S(2)}) async-start(f32[256,1,256]{2,1,0:T(1,128)} %broadcast_in_dim.55), calls=%async_computation | async-start | bytes 524288 | tf_op jit(solution)/shard_map/all_to_all | solution.py:580
  113.2 0.9 copy-done.1
  114.2 0.7 finish.1
  114.9 2.3 %collective-permute-start.12 = (bf16[2,2,128,128]{3,2,1,0:T(8,128)(2,1)S(1)}, bf16[2,2,128,128]{3,2,1,0:T(8,128)(2,1)S(1)}, u32[]{:S(2)}, u32[]{:S(2)}) collective-permute-start(bf16[2,2,128,128]{3,2,1,0:T(8,128)(2,1)S(1)} %get-tuple-element.45), channel_id=1, source_target_pairs={{0,1},{1,0},{2,3},{3,2},{4,5},{5,4},{6,7},{7,6},{8,9},{9,8},{10,11... | collective-permute-start | bytes 393224 | tf_op jit(solution)/shard_map/ppermute | solution.py:532
  117.3 0.8 collective-permute-done.12
  118.3 0.8 copy.54
  119.0 0.8 copy.53
  119.8 8.3 %all-to-all-done = f32[256,1,256]{2,1,0:T(1,128)} async-done(((f32[256,1,256]{2,1,0:T(1,128)}), f32[256,1,256]{2,1,0:T(1,128)}, u32[]{:S(2)}, u32[]{:S(2)}) %all-to-all-start) | async-done | bytes 262176 | tf_op jit(solution)/shard_map/all_to_all | solution.py:580
  128.1 1.2 reduce_sum.19
  129.4 0.5 fusion.5
  130.1 1.6 %copy.52 = bf16[128,32,128]{2,1,0:T(8,128)(2,1)} copy(bf16[128,32,128]{2,0,1:T(8,128)(2,1)S(1)} %maximum_bitcast_fusion) | data formatting | bytes 2097152
  (58 shorter events, 1.7 us)
Async XLA Ops:
  0.6 4.6 %copy-start.5 = (bf16[128,32,128]{2,1,0:T(8,128)(2,1)S(1)}, bf16[128,32,128]{2,1,0:T(8,128)(2,1)}, u32[]{:S(2)}) copy-start(bf16[128,32,128]{2,1,0:T(8,128)(2,1)} %param.9) | copy-start | bytes 3145732
  1.8 4.7 %copy-start.6 = (bf16[128,32,128]{2,1,0:T(8,128)(2,1)S(1)}, bf16[128,32,128]{2,1,0:T(8,128)(2,1)}, u32[]{:S(2)}) copy-start(bf16[128,32,128]{2,1,0:T(8,128)(2,1)} %param.12) | copy-start | bytes 3145732
  1.9 7.2 %collective-permute-start.2 = (bf16[2,2,128,128]{3,2,1,0:T(8,128)(2,1)S(1)}, bf16[2,2,128,128]{3,2,1,0:T(8,128)(2,1)S(1)}, u32[]{:S(2)}, u32[]{:S(2)}) collective-permute-start(bf16[2,2,128,128]{3,2,1,0:T(8,128)(2,1)S(1)} %bitcast.65), channel_id=1, source_target_pairs={{0,1},{1,0},{2,3},{3,2},{4,5},{5,4},{6,7},{7,6},{8,9},{9,8},{10,11... | collective-permute-start | bytes 393224 | tf_op jit(solution)/shard_map/ppermute | solution.py:532
  5.6 2.7 %copy-start.3 = (s32[1,8]{1,0:T(1,128)S(1)}, s32[1,8]{1,0:T(1,128)}, u32[]{:S(2)}) copy-start(s32[1,8]{1,0:T(1,128)} %lens.5) | copy-start | bytes 100
  5.6 3.0 %copy-start.7 = (s32[16,8]{0,1:T(8,128)S(1)}, s32[16,8]{0,1:T(8,128)}, u32[]{:S(2)}) copy-start(s32[16,8]{0,1:T(8,128)} %param.16) | copy-start | bytes 1540
  5.6 3.2 %copy-start.8 = (s32[16,8]{0,1:T(8,128)S(1)}, s32[16,8]{0,1:T(8,128)}, u32[]{:S(2)}) copy-start(s32[16,8]{0,1:T(8,128)} %param.17) | copy-start | bytes 1540
  6.5 21.3 %collective-permute-start = (bf16[16,128,128]{2,1,0:T(8,128)(2,1)}, bf16[16,128,128]{2,1,0:T(8,128)(2,1)}, u32[]{:S(2)}, u32[]{:S(2)}) collective-permute-start(bf16[16,128,128]{2,1,0:T(8,128)(2,1)} %dynamic-slice_bitcast_fusion.1), channel_id=1, source_target_pairs={{0,1},{1,0},{2,3},{3,2},{4,5},{5,4},{6,7},{7,6},{8,9},{9,8},{10,11... | collective-permute-start | bytes 1572872 | tf_op jit(solution)/shard_map/ppermute | solution.py:532
  6.5 21.3 %copy-start.2 = (f32[128]{0:T(128)S(1)}, f32[128]{0:T(128)}, u32[]{:S(2)}) copy-start(f32[128]{0:T(128)} %param.14) | copy-start | bytes 1540
  6.5 21.3 %copy-start.4 = (f32[128]{0:T(128)S(1)}, f32[128]{0:T(128)}, u32[]{:S(2)}) copy-start(f32[128]{0:T(128)} %param.13) | copy-start | bytes 1540
  7.8 20.1 %collective-permute-start.1 = (bf16[16,128,128]{2,1,0:T(8,128)(2,1)}, bf16[16,128,128]{2,1,0:T(8,128)(2,1)}, u32[]{:S(2)}, u32[]{:S(2)}) collective-permute-start(bf16[16,128,128]{2,1,0:T(8,128)(2,1)} %dynamic-slice_bitcast_fusion), channel_id=1, source_target_pairs={{0,1},{1,0},{2,3},{3,2},{4,5},{5,4},{6,7},{7,6},{8,9},{9,8},{10,11... | collective-permute-start | bytes 1572872 | tf_op jit(solution)/shard_map/ppermute | solution.py:532
  9.1 17.2 %collective-permute-start.4 = (bf16[2,2,2,128,128]{4,3,2,1,0:T(8,128)(2,1)S(1)}, bf16[2,2,2,128,128]{4,3,2,1,0:T(8,128)(2,1)S(1)}, u32[]{:S(2)}, u32[]{:S(2)}) collective-permute-start(bf16[2,2,2,128,128]{4,3,2,1,0:T(8,128)(2,1)S(1)} %pad_maximum_fusion.1.kv.kv0), channel_id=1, source_target_pairs={{0,2},{1,3},{2,4},{3,5},{4,6},{5,7},{6,8},{7,9},{8,10},{9,11},{10,... | collective-permute-start | bytes 786440 | tf_op jit(solution)/shard_map/ppermute | solution.py:536
  18.6 16.5 %collective-permute-start.6 = (bf16[2,2,2,128,128]{4,3,2,1,0:T(8,128)(2,1)S(1)}, bf16[2,2,2,128,128]{4,3,2,1,0:T(8,128)(2,1)S(1)}, u32[]{:S(2)}, u32[]{:S(2)}) collective-permute-start(bf16[2,2,2,128,128]{4,3,2,1,0:T(8,128)(2,1)S(1)} %pad_maximum_fusion.1.kv.kv0), channel_id=1, source_target_pairs={{0,4},{1,5},{2,6},{3,7},{4,8},{5,9},{6,10},{7,11},{8,12},{9,13},{1... | collective-permute-start | bytes 786440 | tf_op jit(solution)/shard_map/ppermute | solution.py:536
  21.8 13.3 %collective-permute-start.3 = (bf16[2,2,2,128,128]{4,3,2,1,0:T(8,128)(2,1)S(1)}, bf16[2,2,2,128,128]{4,3,2,1,0:T(8,128)(2,1)S(1)}, u32[]{:S(2)}, u32[]{:S(2)}) collective-permute-start(bf16[2,2,2,128,128]{4,3,2,1,0:T(8,128)(2,1)S(1)} %pad_maximum_fusion.1.kv.kv0), channel_id=1, source_target_pairs={{0,8},{1,9},{2,10},{3,11},{4,12},{5,13},{6,14},{7,15},{16,24},{17,... | collective-permute-start | bytes 786440 | tf_op jit(solution)/shard_map/ppermute | solution.py:536
  26.3 13.6 %collective-permute-start.5 = (bf16[2,2,2,128,128]{4,3,2,1,0:T(8,128)(2,1)S(1)}, bf16[2,2,2,128,128]{4,3,2,1,0:T(8,128)(2,1)S(1)}, u32[]{:S(2)}, u32[]{:S(2)}) collective-permute-start(bf16[2,2,2,128,128]{4,3,2,1,0:T(8,128)(2,1)S(1)} %collective-permute-done.4.kv1), channel_id=1, source_target_pairs={{0,4},{1,5},{2,6},{3,7},{4,8},{5,9},{6,10},{7,11},{8,12},{9,13},{1... | collective-permute-start | bytes 786440 | tf_op jit(solution)/shard_map/ppermute | solution.py:536
  56.8 0.7 copy-start
  57.5 55.6 %collective-permute-start.8 = (s16[1040,128]{1,0:T(8,128)(2,1)}, s16[1040,128]{1,0:T(8,128)(2,1)S(1)}, u32[]{:S(2)}, u32[]{:S(2)}) collective-permute-start(s16[1040,128]{1,0:T(8,128)(2,1)} %get-tuple-element.40), channel_id=1, source_target_pairs={{2,0},{3,1},{4,2},{5,3},{6,4},{7,5},{8,6},{9,7},{10,8},{11,9},{12,... | collective-permute-start | bytes 798728 | tf_op jit(solution)/shard_map/ppermute | solution.py:536
  58.8 54.4 %collective-permute-start.9 = (s16[1040,128]{1,0:T(8,128)(2,1)}, s16[1040,128]{1,0:T(8,128)(2,1)S(1)}, u32[]{:S(2)}, u32[]{:S(2)}) collective-permute-start(s16[1040,128]{1,0:T(8,128)(2,1)} %get-tuple-element.41), channel_id=1, source_target_pairs={{4,0},{5,1},{6,2},{7,3},{8,4},{9,5},{10,6},{11,7},{12,8},{13,9},{1... | collective-permute-start | bytes 798728 | tf_op jit(solution)/shard_map/ppermute | solution.py:536
  60.1 53.1 %collective-permute-start.10 = (s16[1040,128]{1,0:T(8,128)(2,1)}, s16[1040,128]{1,0:T(8,128)(2,1)S(1)}, u32[]{:S(2)}, u32[]{:S(2)}) collective-permute-start(s16[1040,128]{1,0:T(8,128)(2,1)} %get-tuple-element.42), channel_id=1, source_target_pairs={{6,0},{7,1},{8,2},{9,3},{10,4},{11,5},{12,6},{13,7},{14,8},{15,9},... | collective-permute-start | bytes 798728 | tf_op jit(solution)/shard_map/ppermute | solution.py:536
  61.4 51.8 %collective-permute-start.11 = (s16[1040,128]{1,0:T(8,128)(2,1)}, s16[1040,128]{1,0:T(8,128)(2,1)S(1)}, u32[]{:S(2)}, u32[]{:S(2)}) collective-permute-start(s16[1040,128]{1,0:T(8,128)(2,1)} %get-tuple-element.43), channel_id=1, source_target_pairs={{8,0},{9,1},{10,2},{11,3},{12,4},{13,5},{14,6},{15,7},{24,16},{25,... | collective-permute-start | bytes 798728 | tf_op jit(solution)/shard_map/ppermute | solution.py:536
  63.6 64.5 %all-to-all-start = ((f32[256,1,256]{2,1,0:T(1,128)}), f32[256,1,256]{2,1,0:T(1,128)}, u32[]{:S(2)}, u32[]{:S(2)}) async-start(f32[256,1,256]{2,1,0:T(1,128)} %broadcast_in_dim.55), calls=%async_computation | async-start | bytes 524288 | tf_op jit(solution)/shard_map/all_to_all | solution.py:580
  113.2 1.0 copy-start.1
  114.9 3.3 %collective-permute-start.12 = (bf16[2,2,128,128]{3,2,1,0:T(8,128)(2,1)S(1)}, bf16[2,2,128,128]{3,2,1,0:T(8,128)(2,1)S(1)}, u32[]{:S(2)}, u32[]{:S(2)}) collective-permute-start(bf16[2,2,128,128]{3,2,1,0:T(8,128)(2,1)S(1)} %get-tuple-element.45), channel_id=1, source_target_pairs={{0,1},{1,0},{2,3},{3,2},{4,5},{5,4},{6,7},{7,6},{8,9},{9,8},{10,11... | collective-permute-start | bytes 393224 | tf_op jit(solution)/shard_map/ppermute | solution.py:532
  117.2 12.7 %collective-permute-start.7 = (bf16[16,128,128]{2,1,0:T(8,128)(2,1)S(1)}, bf16[16,128,128]{2,1,0:T(8,128)(2,1)S(1)}, u32[]{:S(2)}, u32[]{:S(2)}) collective-permute-start(bf16[16,128,128]{2,1,0:T(8,128)(2,1)S(1)} %slice_bitcast_fusion), channel_id=1, source_target_pairs={{0,1},{1,0},{2,3},{3,2},{4,5},{5,4},{6,7},{7,6},{8,9},{9,8},{10,11... | collective-permute-start | bytes 1572872 | tf_op jit(solution)/shard_map/ppermute | solution.py:532
